TPU v7x, 512 devices: a whole 4x8x8 slice. The times are simulated.
512 devices in a mesh: tm: 64 (over y, x, core), chan: 8 (over z).
Axes of the slice: x: 4, y: 8, z: 8, core: 2. Of those that a mesh axis runs over, the one named last changes fastest.
Arguments:
- frames: bfloat16 [64, 512, 1024], P('tm', 'chan'), may hold values from -6 to 6
- decay_rate: float32 [256], P('chan'), may hold values from 0.003125 to 0.1
- step_size: float32 [64], P('tm'), may hold values from 0.5 to 103.9
- in_kernel: bfloat16 [9, 256, 512], replicated, may hold values from -0.09375 to 0.09375
- out_kernel: bfloat16 [9, 512, 256], P(None, 'chan'), may hold values from -0.125 to 0.125
- skip_gain: float32 [512], P('chan'), may hold values from 0.5 to 1.5
Outputs:
- outputs: bfloat16 [64, 512, 1024], P('tm', 'chan')
All inputs are finite; a program needn't handle non-finite values.
Results may differ from a plain program's by a relative error of at most 0.013.
Values may be sent and summed in bfloat16 or wider, within the bound.
No kernel may reach another device: no remote copies, remote signals or barrier semaphores. Data moves between devices by JAX's collectives and lax.ppermute only.
A program may use at most 64 MiB of HBM per device.

v0:
```python
import jax
import jax.numpy as jnp
from jax import lax
from jax.sharding import PartitionSpec as P

GRID_W = 32


def shift_sum(stacked, axis, grid_w):
    cells = stacked.shape[-1]
    margin = grid_w + 1
    widths = [(0, 0)] * (stacked.ndim - 1) + [(margin, margin)]
    padded = jnp.pad(stacked, widths)
    column = jnp.arange(cells) % grid_w
    total = None
    for offset in range(9):
        row_step = offset // 3 - 1
        col_step = offset % 3 - 1
        begin_at = margin + row_step * grid_w + col_step
        taken = lax.index_in_dim(padded, offset, axis, keepdims=False)
        moved = taken[..., begin_at : begin_at + cells]
        inside = ((column + col_step >= 0) & (column + col_step < grid_w)).astype(moved.dtype)
        total = moved * inside if total is None else total + moved * inside
    return total


def advance_block(driven, rates, step_size):
    decay = jnp.exp(-rates[:, None] * step_size[None, :])
    inject = jnp.sqrt(1.0 - decay * decay)
    through = jnp.cumprod(decay, axis=1)
    state = jnp.zeros((driven.shape[0], driven.shape[2]), jnp.float32)
    state = decay * state + inject * driven[:, 0]
    history = [state]
    local = jnp.stack(history, axis=1)
    decays, finals = (
        lax.all_gather(through[:, -1][None], "tm", axis=0, tiled=True),
        lax.all_gather(state[None], "tm", axis=0, tiled=True),
    )
    time_at = lax.axis_index("tm")

    def absorb(source, running):
        moved = decays[source][:, None] * running + finals[source]
        return jnp.where(source < time_at, moved, running)

    carried = lax.fori_loop(0, decays.shape[0], absorb, jnp.zeros_like(state))
    return (local + through[:, :, None] * carried[:, None, :]).astype(jnp.bfloat16)


def body(frames, decay_rate, step_size, in_kernel, out_kernel, skip_gain):
    t_count, u_local, cells = frames.shape
    p_local = decay_rate.shape[0]
    width_all = in_kernel.shape[2]
    state_all = in_kernel.shape[1]
    chan_at = lax.axis_index("chan")
    mine = lax.dynamic_slice_in_dim(in_kernel, chan_at * p_local, p_local, 1).reshape(
        9 * p_local, width_all
    )
    weights = mine
    summed = jnp.einsum(
        "ku,tuc->ktc",
        weights,
        lax.all_gather(frames, "chan", axis=1, tiled=True),
        preferred_element_type=jnp.float32,
    )
    driven = shift_sum(summed.reshape(9, p_local, t_count, cells), 0, GRID_W)
    rounded = advance_block(driven, decay_rate, step_size)
    out_flat = out_kernel.reshape(9 * u_local, state_all)
    weights = out_flat
    summed_out = jnp.einsum(
        "kp,ptc->tkc",
        weights,
        lax.all_gather(rounded, "chan", axis=0, tiled=True),
        preferred_element_type=jnp.float32,
    )
    mixed = shift_sum(summed_out.reshape(t_count, 9, u_local, cells), 1, GRID_W)
    mixed = mixed + skip_gain[None, :, None] * frames.astype(jnp.float32)
    return jax.nn.gelu(mixed).astype(jnp.bfloat16)


def solution(mesh):
    in_specs = (P("tm", "chan", None), P("chan"), P("tm"), P(), P(None, "chan", None), P("chan"))
    out_specs = P("tm", "chan", None)
    return jax.shard_map(body, mesh=mesh, in_specs=in_specs, out_specs=out_specs, check_vma=False)
```

profile of v0, /device:TPU:64, one launch (start us, length us, event | category | flops | bytes accessed | tf_op | source)
XLA Modules:
  0.0 287.9 jit_solution(10438405218218644889)
XLA Ops:
  8.7 46.1 %all-gather.5.cloned.1.call-done = bf16[1,512,1024]{2,1,0:T(8,128)(2,1)} async-done(((bf16[1,64,1024]{2,1,0:T(8,128)(2,1)}), bf16[1,512,1024]{2,1,0:T(8,128)(2,1)}) %all-gather.5.cloned.1.call-update) | async-done | bytes 1048592 | tf_op jit(solution)/shard_map/all_gather | solution.py:62
  54.8 1.7 convolution_bitcast_fusion
  57.1 1.0 fusion.38
  58.2 1.3 dynamic-slice
  60.4 126.8 %all-reduce.2 = f32[2048]{0:T(1024)S(1)} all-reduce(f32[2048]{0:T(1024)S(1)} %dynamic-update-slice), channel_id=2, replica_groups=mesh['tm'=64,'chan'=8] {'tm'}, use_global_device_ids=true, to_apply=%add.2 | all-reduce | flops 2048 | bytes 16384
  187.3 66.1 %while.14 = (s32[]{:T(128)}, f32[32,1024]{1,0:T(8,128)S(1)}, s32[]{:T(128)}, f32[64,32]{1,0:T(8,128)S(1)}, f32[64,32,1024]{2,1,0:T(8,128)}, /*index=5*/s32[]{:T(128)}, s32[]{:T(128)}) while((s32[]{:T(128)}, f32[32,1024]{1,0:T(8,128)S(1)}, s32[]{:T(128)}, f32[64,32]{1,0:T(8,128)S(1)}, f32[64,32,1024]{2,1,0:T(8,128)}, ...), condition=%wide.region_2.3_spmd.clone, body=%wide.region_1.2_spmd.clone.sunk | while | flops 131076 | bytes 393705 | solution.py:45
  187.3 1.0 fusion.66
  188.3 1.0 fusion.66
  189.4 1.0 fusion.66
  190.4 1.0 fusion.66
  191.4 1.0 fusion.66
  192.5 1.0 fusion.66
  193.5 1.0 fusion.66
  194.5 1.0 fusion.66
  195.6 1.0 fusion.66
  196.6 1.0 fusion.66
  197.6 1.0 fusion.66
  198.7 1.0 fusion.66
  199.7 1.0 fusion.66
  200.7 1.0 fusion.66
  201.8 1.0 fusion.66
  202.8 1.0 fusion.66
  203.8 1.0 fusion.66
  204.9 1.0 fusion.66
  205.9 1.0 fusion.66
  206.9 1.0 fusion.66
  208.0 1.0 fusion.66
  209.0 1.0 fusion.66
  210.0 1.0 fusion.66
  211.1 1.0 fusion.66
  212.1 1.0 fusion.66
  213.1 1.0 fusion.66
  214.2 1.0 fusion.66
  215.2 1.0 fusion.66
  216.2 1.0 fusion.66
  217.3 1.0 fusion.66
  218.3 1.0 fusion.66
  219.3 1.0 fusion.66
  220.4 1.0 fusion.66
  221.4 1.0 fusion.66
  222.4 1.0 fusion.66
  223.5 1.0 fusion.66
  224.5 1.0 fusion.66
  225.5 1.0 fusion.66
  226.6 1.0 fusion.66
  227.6 1.0 fusion.66
  228.6 1.0 fusion.66
  229.7 1.0 fusion.66
  230.7 1.0 fusion.66
  231.7 1.0 fusion.66
  232.8 1.0 fusion.66
  233.8 1.0 fusion.66
  234.8 1.0 fusion.66
  235.9 1.0 fusion.66
  239.0 1.0 fusion.66
  240.0 1.0 fusion.66
  243.1 1.0 fusion.66
  244.1 1.0 fusion.66
  245.2 1.0 fusion.66
  248.3 1.0 fusion.66
  249.3 1.0 fusion.66
  250.3 1.0 fusion.66
  253.5 24.9 %all-gather.1 = bf16[256,1024]{1,0:T(8,128)(2,1)S(1)} all-gather(bf16[32,1024]{1,0:T(8,128)(2,1)S(1)} %fusion.41), channel_id=3, replica_groups=mesh['tm'=64,'chan'=8] {'chan'}, dimensions={0}, use_global_device_ids=true | all-gather | bytes 589824 | tf_op jit(solution)/shard_map/all_gather | solution.py:72
  279.8 1.3 fusion.19
  (100 shorter events, 12.4 us)
Async XLA Ops:
  6.5 48.3 %copy-start = (bf16[9,256,512]{2,1,0:T(8,128)(2,1)S(1)}, bf16[9,256,512]{2,1,0:T(8,128)(2,1)}, u32[]{:S(2)}) copy-start(bf16[9,256,512]{2,1,0:T(8,128)(2,1)} %param.11) | copy-start | bytes 7077892
  6.5 48.3 %all-gather.5.cloned.1.call-start = ((), (), s32[]{:S(2)}) async-start(), calls=%async_computation | async-start | bytes 1179648 | tf_op jit(solution)/shard_map/all_gather | solution.py:62
  7.3 180.0 %all-gather.7.cloned.1.call-start = ((), (), s32[]{:S(2)}) async-start(), calls=%async_computation.1 | async-start | bytes 8519680 | tf_op jit(solution)/shard_map/all_gather | solution.py:37
  57.1 221.3 %copy-start.2 = (bf16[9,64,256]{2,1,0:T(8,128)(2,1)S(1)}, bf16[9,64,256]{2,1,0:T(8,128)(2,1)}, u32[]{:S(2)}) copy-start(bf16[9,64,256]{2,1,0:T(8,128)(2,1)} %param.12) | copy-start | bytes 884740
  278.9 0.9 copy-start.1
  278.9 0.9 copy-start.3
Sparse Core Ops, SparseCore 0:
  9.4 45.3 all-gather.4
  58.3 87.1 all-gather.6
where the time goes:
time: 291 us; the launch traced here: 288 us
  blocking collectives  152 us (52%)
  other arithmetic  66.6 us (23%)
  waiting for transfers between devices  46.9 us (16%)
  between operations  14.8 us (5%)
  local copies, waits for them, and re-layouts  3.77 us (1%)
    unnamed x1, blocking collectives  127 us
    select_n x64, other arithmetic, absorb(): return jnp.where(source < time_at, moved, running)  63.5 us
    all_gather x1, waiting for transfers between devices, body(): lax.all_gather(frames, 'chan', axis=1, tiled=True)  46.1 us
    all_gather x1, blocking collectives, body(): lax.all_gather(rounded, 'chan', axis=0, tiled=True)  24.9 us
  transfers between devices with their start and end apart: 2, of which 1 were waited for; matrix products, arithmetic and copies ran while one was open for 1% of the time, Pallas kernels for 0%

commit v1 on v0

v1 whole, which is shorter than its diff:
```python
import functools

import jax
import jax.numpy as jnp
from jax import lax
from jax.experimental import pallas as pl
from jax.experimental.pallas import tpu as pltpu
from jax.sharding import Mesh, PartitionSpec as P

ROW = 32
TILE = 128
BF = jnp.bfloat16
F32 = jnp.float32


def lanes_of(shape):
    return lax.broadcasted_iota(jnp.int32, shape, len(shape) - 1)


def roll_lanes(x, by):
    return pltpu.roll(x, by % x.shape[-1], len(x.shape) - 1)


def to_column(row):
    n = row.shape[-1]
    eye = lax.broadcasted_iota(jnp.int32, (n, n), 0) == lax.broadcasted_iota(jnp.int32, (n, n), 1)
    return jnp.sum(jnp.where(eye, jnp.broadcast_to(row, (n, n)), 0.0), axis=1, keepdims=True)


def pieces(column):
    high = column.astype(BF).astype(F32)
    rest = column - high
    mid = rest.astype(BF).astype(F32)
    return high, mid, rest - mid


def spread(column, at, shape):
    lane = lanes_of(shape)
    tile = jnp.zeros(shape, F32)
    for n, piece in enumerate(pieces(column)):
        tile = jnp.where(lane == at + n, piece, tile)
    return tile


def collect(tile, at):
    lane = lanes_of(tile.shape)
    inside = (lane >= at) & (lane < at + 3)
    return jnp.sum(jnp.where(inside, tile.astype(F32), 0.0), axis=-1, keepdims=True)


def call(kernel, outs, *operands, smem=(), vmem=32):
    specs = [
        pl.BlockSpec(memory_space=pltpu.SMEM if n in smem else pltpu.VMEM) for n in range(len(operands))
    ]
    return pl.pallas_call(
        kernel,
        out_shape=outs,
        in_specs=specs,
        out_specs=pl.BlockSpec(memory_space=pltpu.VMEM),
        compiler_params=pltpu.CompilerParams(vmem_limit_bytes=vmem << 20),
    )(*operands)


def cut_rows(frame_ref, rate_ref, out_ref):
    blocks = out_ref.shape[0]
    channels = out_ref.shape[1]
    lane = lanes_of((channels, TILE))
    own = to_column(rate_ref[...])
    column = jnp.concatenate([own, jnp.zeros((channels - own.shape[0], 1), F32)], axis=0)
    meta = spread(column, ROW, (channels, TILE))
    for b in range(blocks):
        out_ref[b, :, :TILE] = frame_ref[:, b * TILE : (b + 1) * TILE]
        side = meta
        if b + 1 < blocks:
            after = frame_ref[:, (b + 1) * TILE : (b + 2) * TILE].astype(F32)
            side = jnp.where(lane < ROW, after, side)
        if b > 0:
            before = frame_ref[:, (b - 1) * TILE : b * TILE].astype(F32)
            side = jnp.where(lane >= TILE - ROW, before, side)
        out_ref[b, :, TILE:] = side.astype(BF)


def drive(step_ref, rows_ref, weight_ref, out_ref):
    blocks, channels, _ = rows_ref.shape
    states = weight_ref.shape[1]
    main = rows_ref[:, :, :TILE].reshape(blocks * channels, TILE)
    side = rows_ref[:, :, TILE:].reshape(blocks * channels, TILE)
    lane = lanes_of(main.shape)
    column = lanes_of((states, TILE)) % ROW
    total = None
    for i in range(3):
        if i == 0:
            source = jnp.where(lane >= TILE - ROW, side, main)
        elif i == 2:
            source = jnp.where(lane < ROW, side, main)
        else:
            source = main
        row = jnp.dot(weight_ref[3 * i + 1], source, preferred_element_type=F32)
        left = jnp.dot(weight_ref[3 * i], source, preferred_element_type=F32)
        right = jnp.dot(weight_ref[3 * i + 2], source, preferred_element_type=F32)
        row = row + jnp.where(column > 0, roll_lanes(left, 1), 0.0)
        row = row + jnp.where(column < ROW - 1, roll_lanes(right, -1), 0.0)
        row = roll_lanes(row, (1 - i) * ROW) if i != 1 else row
        total = row if total is None else total + row
    own = states // blocks
    rate = jnp.concatenate([collect(rows_ref[b, :own, TILE:], ROW) for b in range(blocks)], axis=0)
    decay = jnp.exp(-rate * step_ref[0])
    inject = jnp.sqrt(1.0 - decay * decay)
    scaled = (inject * total).astype(BF)
    meta = spread(decay, 0, (states, TILE)).astype(BF)
    group, part, _ = out_ref.shape
    for g in range(group):
        out_ref[g, :, :TILE] = scaled[g * part : (g + 1) * part]
        out_ref[g, :, TILE:] = meta[g * part : (g + 1) * part]


def finish_group(driven_ref, out_ref):
    frames, part, _ = driven_ref.shape
    state = None
    through = None
    for f in range(frames):
        decay = collect(driven_ref[f, :, TILE:], 0)
        value = driven_ref[f, :, :TILE].astype(F32)
        state = value if f == 0 else decay * state + value
        through = decay if f == 0 else decay * through
    final = state.astype(BF)
    meta = spread(through, 0, (part, TILE)).astype(BF)
    for g in range(out_ref.shape[0]):
        out_ref[g, :, :TILE] = final
        out_ref[g, :, TILE:] = meta


def run_group(at_ref, final_ref, driven_ref, out_ref):
    groups = final_ref.shape[0]
    frames, part, _ = driven_ref.shape
    at = at_ref[0]
    state = jnp.zeros((part, TILE), F32)
    for g in range(groups):
        through = collect(final_ref[g, :, TILE:], 0)
        moved = through * state + final_ref[g, :, :TILE].astype(F32)
        state = jnp.where(g < at, moved, state)
    copies = out_ref.shape[1]
    for f in range(frames):
        decay = collect(driven_ref[f, :, TILE:], 0)
        state = decay * state + driven_ref[f, :, :TILE].astype(F32)
        rounded = state.astype(BF)
        for c in range(copies):
            out_ref[f, c] = rounded


def finish(state_ref, frame_ref, weight_ref, gain_ref, out_ref):
    groups, blocks, part, _ = state_ref.shape
    states = groups * part
    channels, cells = frame_ref.shape
    tiles = [state_ref[:, b].reshape(states, TILE) for b in range(blocks)]
    lane = lanes_of((states, TILE))
    column = lanes_of((channels, cells)) % ROW
    total = None
    for i in range(3):
        if i == 1:
            source = jnp.concatenate(tiles, axis=1)
        else:
            parts = []
            for b in range(blocks):
                other = b + i - 1
                inside = 0 <= other < blocks
                beside = tiles[other] if inside else jnp.zeros_like(tiles[b])
                edge = lane < ROW if i == 2 else lane >= TILE - ROW
                parts.append(jnp.where(edge, beside, tiles[b]))
            source = jnp.concatenate(parts, axis=1)
        left = jnp.dot(weight_ref[3 * i], source, preferred_element_type=F32)
        row = jnp.dot(weight_ref[3 * i + 1], source, preferred_element_type=F32)
        right = jnp.dot(weight_ref[3 * i + 2], source, preferred_element_type=F32)
        row = row + jnp.where(column > 0, roll_lanes(left, 1), 0.0)
        row = row + jnp.where(column < ROW - 1, roll_lanes(right, -1), 0.0)
        if i != 1:
            row = jnp.concatenate(
                [
                    roll_lanes(row[:, b * TILE : (b + 1) * TILE], (1 - i) * ROW)
                    for b in range(blocks)
                ],
                axis=1,
            )
        total = row if total is None else total + row
    total = total + to_column(gain_ref[...]) * frame_ref[...].astype(F32)
    out_ref[...] = jax.nn.gelu(total).astype(BF)


def body(groups, frames, decay_rate, step_size, in_kernel, out_kernel, skip_gain):
    _, channels, cells = frames.shape
    blocks = cells // TILE
    states = in_kernel.shape[1]
    members = lax.axis_size("xc")
    part = states // members
    frame = frames.reshape(channels, cells)
    shape = jax.ShapeDtypeStruct
    cut = call(cut_rows, shape((blocks, channels, 2 * TILE), BF), frame, decay_rate[None])
    rows = lax.all_to_all(cut, "chan", 0, 0, tiled=True)
    driven = call(
        drive, shape((members, part, 2 * TILE), BF), step_size, rows, in_kernel, smem=(0,)
    )
    driven = lax.all_to_all(driven, "xc", 0, 0, tiled=True)
    final = call(finish_group, shape((groups, part, 2 * TILE), BF), driven)
    final = lax.all_to_all(final, "y", 0, 0, tiled=True)
    at = lax.axis_index("y").reshape(1)
    state = call(
        run_group, shape((members, blocks, part, TILE), BF), at, final, driven, smem=(0,)
    )
    state = state.reshape(members * blocks, part, TILE)
    state = lax.all_to_all(state, ("xc", "chan"), 0, 0, tiled=True)
    state = state.reshape(members, blocks, part, TILE)
    out = call(finish, shape((channels, cells), BF), state, frame, out_kernel, skip_gain[None])
    return out[None]


def solution(mesh):
    groups, members = 8, 8
    fine = Mesh(mesh.devices.reshape(groups, members, mesh.shape["chan"]), ("y", "xc", "chan"))
    time = ("y", "xc")
    in_specs = (P(time, "chan", None), P("chan"), P(time), P(), P(None, "chan", None), P("chan"))
    out_specs = P(time, "chan", None)
    return jax.shard_map(
        functools.partial(body, groups), mesh=fine, in_specs=in_specs, out_specs=out_specs, check_vma=False
    )
```

time: 291 us -> 78.8 us (0.27)
  the two profiles are of different devices: /device:TPU:64 before, /device:TPU:1 now
where the time goes in v1:
time: 78.8 us; the launch traced here: 78.3 us
  blocking collectives  34.7 us (44%)
  starting transfers between devices  17.7 us (22%)
  waiting for transfers between devices  17.6 us (22%)
  Pallas kernels  4.51 us (6%)
  local copies, waits for them, and re-layouts  3.23 us (4%)
    all_to_all x1, blocking collectives, body(): state = lax.all_to_all(state, ('xc', 'chan'), 0, 0, tiled=True)  22.8 us
    all_to_all x1, blocking collectives, body(): driven = lax.all_to_all(driven, 'xc', 0, 0, tiled=True)  11.8 us
    all_to_all x1, starting transfers between devices, body(): rows = lax.all_to_all(cut, 'chan', 0, 0, tiled=True)  10.9 us
    all_to_all x1, waiting for transfers between devices, body(): rows = lax.all_to_all(cut, 'chan', 0, 0, tiled=True)  9.72 us
    all_to_all x1, waiting for transfers between devices, body(): final = lax.all_to_all(final, 'y', 0, 0, tiled=True)  7.85 us
    all_to_all x1, starting transfers between devices, body(): final = lax.all_to_all(final, 'y', 0, 0, tiled=True)  6.82 us
    pallas_call x5, Pallas kernels, call(): pl.pallas_call(kernel, out_shape=outs, in_specs=specs, out_specs=pl.Block...  4.51 us
    unnamed x12, local copies, waits for them, and re-layouts  3.23 us
  transfers between devices with their start and end apart: 2, of which 2 were waited for; matrix products, arithmetic and copies ran while one was open for 0% of the time, Pallas kernels for 0%

profile of v1, /device:TPU:1, one launch (start us, length us, event | category | flops | bytes accessed | tf_op | source)
XLA Modules:
  0.0 78.3 jit_solution(3186190655340806583)
XLA Ops:
  0.0 0.0 copy-start.1
  0.0 0.9 %copy-done.1 = bf16[1,64,1024]{2,1,0:T(8,128)(2,1)S(1)} copy-done((bf16[1,64,1024]{2,1,0:T(8,128)(2,1)S(1)}, bf16[1,64,1024]{2,1,0:T(8,128)(2,1)}, u32[]{:S(2)}) %copy-start.1) | copy-done | bytes 131096
  0.9 0.0 copy-start.4
  0.9 0.7 copy-done.4
  1.6 0.9 %shard_map.64 = bf16[8,64,256]{2,1,0:T(8,128)(2,1)} custom-call(bf16[64,1024]{1,0:T(8,128)(2,1)S(1)} %bitcast.9, f32[1,32]{1,0:T(1,128)S(1)} %bitcast.11), custom_call_target="tpu_custom_call" | custom-call | tf_op jit(solution)/shard_map/pallas_call | solution.py:55
  2.5 10.9 %all-to-all-start = ((bf16[8,64,256]{2,1,0:T(8,128)(2,1)}), bf16[8,64,256]{2,1,0:T(8,128)(2,1)S(1)}, u32[]{:S(2)}, u32[]{:S(2)}) async-start(bf16[8,64,256]{2,1,0:T(8,128)(2,1)} %shard_map.64), calls=%async_computation | async-start | bytes 524288 | tf_op jit(solution)/shard_map/all_to_all | solution.py:198
  14.0 9.7 %all-to-all-done.rows_ref = bf16[8,64,256]{2,1,0:T(8,128)(2,1)S(1)} async-done(((bf16[8,64,256]{2,1,0:T(8,128)(2,1)}), bf16[8,64,256]{2,1,0:T(8,128)(2,1)S(1)}, u32[]{:S(2)}, u32[]{:S(2)}) %all-to-all-start) | async-done | bytes 262176 | tf_op jit(solution)/shard_map/all_to_all | solution.py:198
  23.7 0.0 copy-start
  23.7 1.7 %copy-done = bf16[9,256,512]{2,1,0:T(8,128)(2,1)S(1)} copy-done((bf16[9,256,512]{2,1,0:T(8,128)(2,1)S(1)}, bf16[9,256,512]{2,1,0:T(8,128)(2,1)}, u32[]{:S(2)}) %copy-start) | copy-done | bytes 2359320
  25.4 0.0 copy-start.2
  25.4 0.0 copy-start.3
  25.4 0.0 copy-start.5
  25.4 0.9 %shard_map.65 = bf16[8,32,256]{2,1,0:T(8,128)(2,1)S(1)} custom-call(f32[1]{0:T(128)S(6)} %copy.7.step_ref, bf16[8,64,256]{2,1,0:T(8,128)(2,1)S(1)} %all-to-all-done.rows_ref, bf16[9,256,512]{2,1,0:T(8,128)(2,1)S(1)} %copy-done), custom_call_target="tpu_custom_call" | custom-call | tf_op jit(solution)/shard_map/pallas_call | solution.py:55
  26.3 11.8 %all_to_all.20.driven_ref = bf16[8,32,256]{2,1,0:T(8,128)(2,1)S(1)} all-to-all(bf16[8,32,256]{2,1,0:T(8,128)(2,1)S(1)} %shard_map.65), channel_id=1, replica_groups=mesh['y'=8,'xc'=8,'chan'=8] {'xc'}, dimensions={0} | all-to-all | bytes 262144 | tf_op jit(solution)/shard_map/all_to_all | solution.py:202
  38.1 0.8 shard_map.66
  38.9 6.8 %all-to-all-start.2 = ((bf16[8,32,256]{2,1,0:T(8,128)(2,1)}), bf16[8,32,256]{2,1,0:T(8,128)(2,1)S(1)}, u32[]{:S(2)}, u32[]{:S(2)}) async-start(bf16[8,32,256]{2,1,0:T(8,128)(2,1)} %shard_map.66), calls=%async_computation.2 | async-start | bytes 262144 | tf_op jit(solution)/shard_map/all_to_all | solution.py:204
  45.7 7.9 %all-to-all-done.2.final_ref = bf16[8,32,256]{2,1,0:T(8,128)(2,1)S(1)} async-done(((bf16[8,32,256]{2,1,0:T(8,128)(2,1)}), bf16[8,32,256]{2,1,0:T(8,128)(2,1)S(1)}, u32[]{:S(2)}, u32[]{:S(2)}) %all-to-all-start.2) | async-done | bytes 131104 | tf_op jit(solution)/shard_map/all_to_all | solution.py:204
  53.6 0.1 shard_map.67
  53.7 22.8 %all_to_all.21 = bf16[64,32,128]{2,1,0:T(8,128)(2,1)S(1)} all-to-all(bf16[64,32,128]{2,1,0:T(8,128)(2,1)S(1)} %bitcast.7), channel_id=1, replica_groups=mesh['y'=8,'xc'=8,'chan'=8] {'xc','chan'}, dimensions={0} | all-to-all | bytes 1048576 | tf_op jit(solution)/shard_map/all_to_all | solution.py:210
  76.6 0.0 copy-done.2
  76.6 0.0 copy-done.3
  76.6 0.0 copy-done.5
  76.6 1.8 %shard_map.68 = bf16[64,1024]{1,0:T(8,128)(2,1)} custom-call(bf16[8,8,32,128]{3,2,1,0:T(8,128)(2,1)S(1)} %bitcast.8, bf16[64,1024]{1,0:T(8,128)(2,1)S(1)} %bitcast.10, bf16[9,64,256]{2,1,0:T(8,128)(2,1)S(1)} %copy-done.3, f32[1,64]{1,0:T(1,128)S(1)} %bitcast.12), custom_call_target="tpu_custom_call" | custom-call | tf_op jit(solution)/shard_map/pallas_call | solution.py:55
Async XLA Ops:
  0.0 0.9 %copy-start.1 = (bf16[1,64,1024]{2,1,0:T(8,128)(2,1)S(1)}, bf16[1,64,1024]{2,1,0:T(8,128)(2,1)}, u32[]{:S(2)}) copy-start(bf16[1,64,1024]{2,1,0:T(8,128)(2,1)} %param.6) | copy-start | bytes 393220
  0.9 0.7 copy-start.4
  2.5 21.2 %all-to-all-start = ((bf16[8,64,256]{2,1,0:T(8,128)(2,1)}), bf16[8,64,256]{2,1,0:T(8,128)(2,1)S(1)}, u32[]{:S(2)}, u32[]{:S(2)}) async-start(bf16[8,64,256]{2,1,0:T(8,128)(2,1)} %shard_map.64), calls=%async_computation | async-start | bytes 524288 | tf_op jit(solution)/shard_map/all_to_all | solution.py:198
  23.7 1.7 %copy-start = (bf16[9,256,512]{2,1,0:T(8,128)(2,1)S(1)}, bf16[9,256,512]{2,1,0:T(8,128)(2,1)}, u32[]{:S(2)}) copy-start(bf16[9,256,512]{2,1,0:T(8,128)(2,1)} %weight_ref.2) | copy-start | bytes 7077892
  25.4 51.2 %copy-start.2 = (bf16[1,64,1024]{2,1,0:T(8,128)(2,1)S(1)}, bf16[1,64,1024]{2,1,0:T(8,128)(2,1)}, u32[]{:S(2)}) copy-start(bf16[1,64,1024]{2,1,0:T(8,128)(2,1)} %param.6) | copy-start | bytes 393220
  25.4 51.2 %copy-start.3 = (bf16[9,64,256]{2,1,0:T(8,128)(2,1)S(1)}, bf16[9,64,256]{2,1,0:T(8,128)(2,1)}, u32[]{:S(2)}) copy-start(bf16[9,64,256]{2,1,0:T(8,128)(2,1)} %weight_ref.3) | copy-start | bytes 884740
  25.4 51.2 %copy-start.5 = (f32[64]{0:T(128)S(1)}, f32[64]{0:T(128)}, u32[]{:S(2)}) copy-start(f32[64]{0:T(128)} %param.11) | copy-start | bytes 772
  38.9 14.7 %all-to-all-start.2 = ((bf16[8,32,256]{2,1,0:T(8,128)(2,1)}), bf16[8,32,256]{2,1,0:T(8,128)(2,1)S(1)}, u32[]{:S(2)}, u32[]{:S(2)}) async-start(bf16[8,32,256]{2,1,0:T(8,128)(2,1)} %shard_map.66), calls=%async_computation.2 | async-start | bytes 262144 | tf_op jit(solution)/shard_map/all_to_all | solution.py:204

commit v2 on v1

--- a/solution.py
+++ b/solution.py
@@ -139,51 +139,50 @@
         through = collect(final_ref[g, :, TILE:], 0)
         moved = through * state + final_ref[g, :, :TILE].astype(F32)
         state = jnp.where(g < at, moved, state)
-    copies = out_ref.shape[1]
     for f in range(frames):
         decay = collect(driven_ref[f, :, TILE:], 0)
         state = decay * state + driven_ref[f, :, :TILE].astype(F32)
-        rounded = state.astype(BF)
-        for c in range(copies):
-            out_ref[f, c] = rounded
-
-
-def finish(state_ref, frame_ref, weight_ref, gain_ref, out_ref):
-    groups, blocks, part, _ = state_ref.shape
-    states = groups * part
-    channels, cells = frame_ref.shape
-    tiles = [state_ref[:, b].reshape(states, TILE) for b in range(blocks)]
-    lane = lanes_of((states, TILE))
-    column = lanes_of((channels, cells)) % ROW
-    total = None
+        out_ref[f] = state.astype(BF)
+
+
+def mix(state_ref, weight_ref, out_ref):
+    groups, part, _ = state_ref.shape
+    blocks, _, channels, states = weight_ref.shape
+    source = state_ref[...].reshape(states, TILE)
+    lane = lanes_of((blocks * channels, TILE))
+    column = lane % ROW
+
+    def weight(o):
+        return weight_ref[:, o].reshape(blocks * channels, states)
+
+    rows = []
     for i in range(3):
-        if i == 1:
-            source = jnp.concatenate(tiles, axis=1)
-        else:
-            parts = []
-            for b in range(blocks):
-                other = b + i - 1
-                inside = 0 <= other < blocks
-                beside = tiles[other] if inside else jnp.zeros_like(tiles[b])
-                edge = lane < ROW if i == 2 else lane >= TILE - ROW
-                parts.append(jnp.where(edge, beside, tiles[b]))
-            source = jnp.concatenate(parts, axis=1)
-        left = jnp.dot(weight_ref[3 * i], source, preferred_element_type=F32)
-        row = jnp.dot(weight_ref[3 * i + 1], source, preferred_element_type=F32)
-        right = jnp.dot(weight_ref[3 * i + 2], source, preferred_element_type=F32)
+        left = jnp.dot(weight(3 * i), source, preferred_element_type=F32)
+        row = jnp.dot(weight(3 * i + 1), source, preferred_element_type=F32)
+        right = jnp.dot(weight(3 * i + 2), source, preferred_element_type=F32)
         row = row + jnp.where(column > 0, roll_lanes(left, 1), 0.0)
         row = row + jnp.where(column < ROW - 1, roll_lanes(right, -1), 0.0)
-        if i != 1:
-            row = jnp.concatenate(
-                [
-                    roll_lanes(row[:, b * TILE : (b + 1) * TILE], (1 - i) * ROW)
-                    for b in range(blocks)
-                ],
-                axis=1,
-            )
-        total = row if total is None else total + row
-    total = total + to_column(gain_ref[...]) * frame_ref[...].astype(F32)
-    out_ref[...] = jax.nn.gelu(total).astype(BF)
+        rows.append(row)
+    down = roll_lanes(rows[0], ROW)
+    up = roll_lanes(rows[2], -ROW)
+    main = rows[1] + jnp.where(lane >= ROW, down, 0.0) + jnp.where(lane < TILE - ROW, up, 0.0)
+    side = jnp.where(lane < ROW, down, jnp.where(lane >= TILE - ROW, up, 0.0))
+    out_ref[:, :, :TILE] = main.astype(BF).reshape(blocks, channels, TILE)
+    out_ref[:, :, TILE:] = side.astype(BF).reshape(blocks, channels, TILE)
+
+
+def finish(mixed_ref, frame_ref, gain_ref, out_ref):
+    blocks, channels, _ = mixed_ref.shape
+    lane = lanes_of((channels, TILE))
+    gain = to_column(gain_ref[...])
+    for b in range(blocks):
+        at = slice(b * TILE, (b + 1) * TILE)
+        total = mixed_ref[b, :, :TILE].astype(F32) + gain * frame_ref[:, at].astype(F32)
+        if b > 0:
+            total = total + jnp.where(lane < ROW, mixed_ref[b - 1, :, TILE:].astype(F32), 0.0)
+        if b + 1 < blocks:
+            total = total + jnp.where(lane >= TILE - ROW, mixed_ref[b + 1, :, TILE:].astype(F32), 0.0)
+        out_ref[:, at] = jax.nn.gelu(total).astype(BF)
 
 
 def body(groups, frames, decay_rate, step_size, in_kernel, out_kernel, skip_gain):
@@ -194,6 +193,7 @@
     part = states // members
     frame = frames.reshape(channels, cells)
     shape = jax.ShapeDtypeStruct
+    out_all = lax.all_gather(out_kernel, "chan", axis=0)
     cut = call(cut_rows, shape((blocks, channels, 2 * TILE), BF), frame, decay_rate[None])
     rows = lax.all_to_all(cut, "chan", 0, 0, tiled=True)
     driven = call(
@@ -203,13 +203,11 @@
     final = call(finish_group, shape((groups, part, 2 * TILE), BF), driven)
     final = lax.all_to_all(final, "y", 0, 0, tiled=True)
     at = lax.axis_index("y").reshape(1)
-    state = call(
-        run_group, shape((members, blocks, part, TILE), BF), at, final, driven, smem=(0,)
-    )
-    state = state.reshape(members * blocks, part, TILE)
-    state = lax.all_to_all(state, ("xc", "chan"), 0, 0, tiled=True)
-    state = state.reshape(members, blocks, part, TILE)
-    out = call(finish, shape((channels, cells), BF), state, frame, out_kernel, skip_gain[None])
+    state = call(run_group, shape((members, part, TILE), BF), at, final, driven, smem=(0,))
+    state = lax.all_to_all(state, "xc", 0, 0, tiled=True)
+    mixed = call(mix, shape((blocks, channels, 2 * TILE), BF), state, out_all)
+    mixed = lax.all_to_all(mixed, "chan", 0, 0, tiled=True)
+    out = call(finish, shape((channels, cells), BF), mixed, frame, skip_gain[None])
     return out[None]
 
 

time: 78.8 us -> 94.7 us (1.20)
  between operations: 0.68 us -> 14.1 us
  local copies, waits for them, and re-layouts: 3.23 us -> 4.9 us
    unnamed x12, local copies, waits for them, and re-layouts: 3.23 us -> 4.9 us
    all_to_all x1 -> x2, blocking collectives: 22.8 us -> 22.7 us  [the longest x1 13.1 us: body(): mixed = lax.all_to_all(mixed, 'chan', 0, 0, tiled=True)]
    pallas_call x5 -> x6, Pallas kernels: 4.51 us -> 4.55 us  [call(): pl.pallas_call(kernel, out_shape=outs, in_specs=specs, out_specs=pl.Block...]
  transfers between devices with their start and end apart: 2 -> 3, of which waited for: 2 -> 2; matrix products, arithmetic and copies ran while one was open for 0% -> 0% of each run, Pallas kernels for 0% -> 3%
where the time goes in v2:
time: 94.7 us; the launch traced here: 94.2 us
  blocking collectives  34.7 us (37%)
  waiting for transfers between devices  18.3 us (19%)
  starting transfers between devices  17.6 us (19%)
  between operations  14.1 us (15%)
  local copies, waits for them, and re-layouts  4.9 us (5%)
  Pallas kernels  4.55 us (5%)
    all_to_all x1, blocking collectives, body(): mixed = lax.all_to_all(mixed, 'chan', 0, 0, tiled=True)  13.1 us
    all_to_all x1, blocking collectives, body(): driven = lax.all_to_all(driven, 'xc', 0, 0, tiled=True)  12 us
    all_to_all x1, starting transfers between devices, body(): rows = lax.all_to_all(cut, 'chan', 0, 0, tiled=True)  10.9 us
    all_to_all x1, waiting for transfers between devices, body(): rows = lax.all_to_all(cut, 'chan', 0, 0, tiled=True)  9.72 us
    all_to_all x1, blocking collectives, body(): state = lax.all_to_all(state, 'xc', 0, 0, tiled=True)  9.59 us
    all_to_all x1, waiting for transfers between devices, body(): final = lax.all_to_all(final, 'y', 0, 0, tiled=True)  7.85 us
    all_to_all x1, starting transfers between devices, body(): final = lax.all_to_all(final, 'y', 0, 0, tiled=True)  6.78 us
    unnamed x12, local copies, waits for them, and re-layouts  4.9 us
  transfers between devices with their start and end apart: 3, of which 2 were waited for; matrix products, arithmetic and copies ran while one was open for 0% of the time, Pallas kernels for 3%

profile of v2, /device:TPU:1, one launch (start us, length us, event | category | flops | bytes accessed | tf_op | source)
XLA Modules:
  0.0 94.2 jit_solution(4189941385103641305)
XLA Ops:
  6.5 0.0 all-gather.3.cloned.1.call-start
  6.5 0.7 all-gather.3.cloned.1.call-update
  7.3 0.0 copy-start.2
  7.3 0.9 copy-done.2
  8.2 0.0 copy-start.4
  8.2 0.7 copy-done.4
  8.8 0.9 shard_map.64
  9.7 10.9 %all-to-all-start = ((bf16[8,64,256]{2,1,0:T(8,128)(2,1)}), bf16[8,64,256]{2,1,0:T(8,128)(2,1)S(1)}, u32[]{:S(2)}, u32[]{:S(2)}) async-start(bf16[8,64,256]{2,1,0:T(8,128)(2,1)} %shard_map.64), calls=%async_computation | async-start | bytes 524288 | tf_op jit(solution)/shard_map/all_to_all | solution.py:198
  21.3 9.7 %all-to-all-done.rows_ref = bf16[8,64,256]{2,1,0:T(8,128)(2,1)S(1)} async-done(((bf16[8,64,256]{2,1,0:T(8,128)(2,1)}), bf16[8,64,256]{2,1,0:T(8,128)(2,1)S(1)}, u32[]{:S(2)}, u32[]{:S(2)}) %all-to-all-start) | async-done | bytes 262176 | tf_op jit(solution)/shard_map/all_to_all | solution.py:198
  31.0 0.0 copy-start
  31.0 1.7 %copy-done = bf16[9,256,512]{2,1,0:T(8,128)(2,1)S(1)} copy-done((bf16[9,256,512]{2,1,0:T(8,128)(2,1)S(1)}, bf16[9,256,512]{2,1,0:T(8,128)(2,1)}, u32[]{:S(2)}) %copy-start) | copy-done | bytes 2359320
  32.6 0.9 shard_map.65
  33.6 0.0 copy-start.3
  33.6 0.0 copy-start.5
  33.6 12.0 %all_to_all.25.driven_ref = bf16[8,32,256]{2,1,0:T(8,128)(2,1)S(1)} all-to-all(bf16[8,32,256]{2,1,0:T(8,128)(2,1)S(1)} %shard_map.65), channel_id=1, replica_groups=mesh['y'=8,'xc'=8,'chan'=8] {'xc'}, dimensions={0} | all-to-all | bytes 262144 | tf_op jit(solution)/shard_map/all_to_all | solution.py:202
  45.6 0.8 shard_map.66
  46.4 6.8 %all-to-all-start.2 = ((bf16[8,32,256]{2,1,0:T(8,128)(2,1)}), bf16[8,32,256]{2,1,0:T(8,128)(2,1)S(1)}, u32[]{:S(2)}, u32[]{:S(2)}) async-start(bf16[8,32,256]{2,1,0:T(8,128)(2,1)} %shard_map.66), calls=%async_computation.2 | async-start | bytes 262144 | tf_op jit(solution)/shard_map/all_to_all | solution.py:204
  53.1 7.9 %all-to-all-done.2.final_ref = bf16[8,32,256]{2,1,0:T(8,128)(2,1)S(1)} async-done(((bf16[8,32,256]{2,1,0:T(8,128)(2,1)}), bf16[8,32,256]{2,1,0:T(8,128)(2,1)S(1)}, u32[]{:S(2)}, u32[]{:S(2)}) %all-to-all-start.2) | async-done | bytes 131104 | tf_op jit(solution)/shard_map/all_to_all | solution.py:204
  61.0 0.1 shard_map.67
  61.1 9.6 %all_to_all.26.state_ref = bf16[8,32,128]{2,1,0:T(8,128)(2,1)S(1)} all-to-all(bf16[8,32,128]{2,1,0:T(8,128)(2,1)S(1)} %shard_map.67), channel_id=1, replica_groups=mesh['y'=8,'xc'=8,'chan'=8] {'xc'}, dimensions={0} | all-to-all | bytes 131072 | tf_op jit(solution)/shard_map/all_to_all | solution.py:207
  70.7 0.0 all-gather.3.cloned.1.call-done
  70.7 0.0 copy-start.1
  70.7 1.7 %copy-done.1 = bf16[72,64,256]{2,1,0:T(8,128)(2,1)S(1)} copy-done((bf16[72,64,256]{2,1,0:T(8,128)(2,1)S(1)}, bf16[72,64,256]{2,1,0:T(8,128)(2,1)}, u32[]{:S(2)}) %copy-start.1) | copy-done | bytes 2359320
  72.4 0.9 shard_map.68
  73.3 13.1 %all_to_all.27.mixed_ref = bf16[8,64,256]{2,1,0:T(8,128)(2,1)S(1)} all-to-all(bf16[8,64,256]{2,1,0:T(8,128)(2,1)S(1)} %shard_map.68), channel_id=1, replica_groups=mesh['y'=8,'xc'=8,'chan'=8] {'chan'}, dimensions={0} | all-to-all | bytes 524288 | tf_op jit(solution)/shard_map/all_to_all | solution.py:209
  86.4 0.0 copy-done.3
  86.4 0.0 copy-done.5
  86.4 0.9 shard_map.69
Async XLA Ops:
  6.5 64.2 %all-gather.3.cloned.1.call-start = ((), (), s32[]{:S(2)}) async-start(), calls=%async_computation.5 | async-start | bytes 2654208 | tf_op jit(solution)/shard_map/all_gather | solution.py:196
  7.3 0.9 copy-start.2
  8.2 0.7 copy-start.4
  9.7 21.2 %all-to-all-start = ((bf16[8,64,256]{2,1,0:T(8,128)(2,1)}), bf16[8,64,256]{2,1,0:T(8,128)(2,1)S(1)}, u32[]{:S(2)}, u32[]{:S(2)}) async-start(bf16[8,64,256]{2,1,0:T(8,128)(2,1)} %shard_map.64), calls=%async_computation | async-start | bytes 524288 | tf_op jit(solution)/shard_map/all_to_all | solution.py:198
  31.0 1.7 %copy-start = (bf16[9,256,512]{2,1,0:T(8,128)(2,1)S(1)}, bf16[9,256,512]{2,1,0:T(8,128)(2,1)}, u32[]{:S(2)}) copy-start(bf16[9,256,512]{2,1,0:T(8,128)(2,1)} %weight_ref.1) | copy-start | bytes 7077892
  33.6 52.9 %copy-start.3 = (bf16[1,64,1024]{2,1,0:T(8,128)(2,1)S(1)}, bf16[1,64,1024]{2,1,0:T(8,128)(2,1)}, u32[]{:S(2)}) copy-start(bf16[1,64,1024]{2,1,0:T(8,128)(2,1)} %param.6) | copy-start | bytes 393220
  33.6 52.9 %copy-start.5 = (f32[64]{0:T(128)S(1)}, f32[64]{0:T(128)}, u32[]{:S(2)}) copy-start(f32[64]{0:T(128)} %param.11) | copy-start | bytes 772
  46.4 14.6 %all-to-all-start.2 = ((bf16[8,32,256]{2,1,0:T(8,128)(2,1)}), bf16[8,32,256]{2,1,0:T(8,128)(2,1)S(1)}, u32[]{:S(2)}, u32[]{:S(2)}) async-start(bf16[8,32,256]{2,1,0:T(8,128)(2,1)} %shard_map.66), calls=%async_computation.2 | async-start | bytes 262144 | tf_op jit(solution)/shard_map/all_to_all | solution.py:204
  70.7 1.7 %copy-start.1 = (bf16[72,64,256]{2,1,0:T(8,128)(2,1)S(1)}, bf16[72,64,256]{2,1,0:T(8,128)(2,1)}, u32[]{:S(2)}) copy-start(bf16[72,64,256]{2,1,0:T(8,128)(2,1)} %all-gather.3.cloned.1.call-done) | copy-start | bytes 7077892
Sparse Core Ops, SparseCore 0:
  9.4 47.3 all-gather.2

commit v3 on v1

--- a/solution.py
+++ b/solution.py
@@ -48,24 +48,22 @@
     return jnp.sum(jnp.where(inside, tile.astype(F32), 0.0), axis=-1, keepdims=True)
 
 
-def call(kernel, outs, *operands, smem=(), vmem=32):
-    specs = [
-        pl.BlockSpec(memory_space=pltpu.SMEM if n in smem else pltpu.VMEM) for n in range(len(operands))
-    ]
+def call(kernel, outs, *operands, vmem=32):
+    here = pl.BlockSpec(memory_space=pltpu.VMEM)
     return pl.pallas_call(
         kernel,
         out_shape=outs,
-        in_specs=specs,
-        out_specs=pl.BlockSpec(memory_space=pltpu.VMEM),
+        in_specs=[here] * len(operands),
+        out_specs=here,
         compiler_params=pltpu.CompilerParams(vmem_limit_bytes=vmem << 20),
     )(*operands)
 
 
-def cut_rows(frame_ref, rate_ref, out_ref):
+def cut_rows(frame_ref, pace_ref, out_ref):
     blocks = out_ref.shape[0]
     channels = out_ref.shape[1]
     lane = lanes_of((channels, TILE))
-    own = to_column(rate_ref[...])
+    own = to_column(pace_ref[:, 1:])
     column = jnp.concatenate([own, jnp.zeros((channels - own.shape[0], 1), F32)], axis=0)
     meta = spread(column, ROW, (channels, TILE))
     for b in range(blocks):
@@ -80,7 +78,7 @@
         out_ref[b, :, TILE:] = side.astype(BF)
 
 
-def drive(step_ref, rows_ref, weight_ref, out_ref):
+def drive(pace_ref, rows_ref, weight_ref, out_ref):
     blocks, channels, _ = rows_ref.shape
     states = weight_ref.shape[1]
     main = rows_ref[:, :, :TILE].reshape(blocks * channels, TILE)
@@ -104,7 +102,7 @@
         total = row if total is None else total + row
     own = states // blocks
     rate = jnp.concatenate([collect(rows_ref[b, :own, TILE:], ROW) for b in range(blocks)], axis=0)
-    decay = jnp.exp(-rate * step_ref[0])
+    decay = jnp.exp(-rate * pace_ref[:, :1])
     inject = jnp.sqrt(1.0 - decay * decay)
     scaled = (inject * total).astype(BF)
     meta = spread(decay, 0, (states, TILE)).astype(BF)
@@ -130,10 +128,10 @@
         out_ref[g, :, TILE:] = meta
 
 
-def run_group(at_ref, final_ref, driven_ref, out_ref):
+def run_group(final_ref, driven_ref, out_ref):
     groups = final_ref.shape[0]
     frames, part, _ = driven_ref.shape
-    at = at_ref[0]
+    at = lax.axis_index("y")
     state = jnp.zeros((part, TILE), F32)
     for g in range(groups):
         through = collect(final_ref[g, :, TILE:], 0)
@@ -194,18 +192,14 @@
     part = states // members
     frame = frames.reshape(channels, cells)
     shape = jax.ShapeDtypeStruct
-    cut = call(cut_rows, shape((blocks, channels, 2 * TILE), BF), frame, decay_rate[None])
+    pace = jnp.concatenate([step_size, decay_rate])[None]
+    cut = call(cut_rows, shape((blocks, channels, 2 * TILE), BF), frame, pace)
     rows = lax.all_to_all(cut, "chan", 0, 0, tiled=True)
-    driven = call(
-        drive, shape((members, part, 2 * TILE), BF), step_size, rows, in_kernel, smem=(0,)
-    )
+    driven = call(drive, shape((members, part, 2 * TILE), BF), pace, rows, in_kernel)
     driven = lax.all_to_all(driven, "xc", 0, 0, tiled=True)
     final = call(finish_group, shape((groups, part, 2 * TILE), BF), driven)
     final = lax.all_to_all(final, "y", 0, 0, tiled=True)
-    at = lax.axis_index("y").reshape(1)
-    state = call(
-        run_group, shape((members, blocks, part, TILE), BF), at, final, driven, smem=(0,)
-    )
+    state = call(run_group, shape((members, blocks, part, TILE), BF), final, driven)
     state = state.reshape(members * blocks, part, TILE)
     state = lax.all_to_all(state, ("xc", "chan"), 0, 0, tiled=True)
     state = state.reshape(members, blocks, part, TILE)

time: 78.8 us -> 77.7 us (0.986)
  blocking collectives: 34.7 us -> 70.2 us
  starting transfers between devices: 17.7 us -> 0 us
  waiting for transfers between devices: 17.6 us -> 0 us
  Pallas kernels: 4.51 us -> 3.22 us
    all_to_all x0 -> x2, blocking collectives: none -> 35.5 us  [the longest x1 21 us: body(): rows = lax.all_to_all(cut, 'chan', 0, 0, tiled=True)]
    all_to_all x2 -> x0, starting transfers between devices: 17.7 us -> none  [the longest x1 10.9 us: body(): rows = lax.all_to_all(cut, 'chan', 0, 0, tiled=True)]
    all_to_all x2 -> x0, waiting for transfers between devices: 17.6 us -> none  [the longest x1 9.72 us: body(): rows = lax.all_to_all(cut, 'chan', 0, 0, tiled=True)]
    pallas_call x5, Pallas kernels: 4.51 us -> 3.22 us  [call(): pl.pallas_call(kernel, out_shape=outs, in_specs=[here] * len(operands), o...]
    unnamed x12 -> x10, local copies, waits for them, and re-layouts: 3.23 us -> 2.58 us
  transfers between devices with their start and end apart: 2 -> 0, of which waited for: 2 -> 0; matrix products, arithmetic and copies ran while one was open for 0% -> 0% of each run, Pallas kernels for 0% -> 0%
where the time goes in v3:
time: 77.7 us; the launch traced here: 77.4 us
  blocking collectives  70.2 us (90%)
  Pallas kernels  3.22 us (4%)
  local copies, waits for them, and re-layouts  2.58 us (3%)
    all_to_all x1, blocking collectives, body(): state = lax.all_to_all(state, ('xc', 'chan'), 0, 0, tiled=True)  22.8 us
    all_to_all x1, blocking collectives, body(): rows = lax.all_to_all(cut, 'chan', 0, 0, tiled=True)  21 us
    all_to_all x1, blocking collectives, body(): final = lax.all_to_all(final, 'y', 0, 0, tiled=True)  14.5 us
    all_to_all x1, blocking collectives, body(): driven = lax.all_to_all(driven, 'xc', 0, 0, tiled=True)  11.8 us
    pallas_call x5, Pallas kernels, call(): pl.pallas_call(kernel, out_shape=outs, in_specs=[here] * len(operands), o...  3.22 us
    unnamed x10, local copies, waits for them, and re-layouts  2.58 us

profile of v3, /device:TPU:1, one launch (start us, length us, event | category | flops | bytes accessed | tf_op | source)
XLA Modules:
  0.0 77.4 jit_solution(1208357846179954957)
XLA Ops:
  0.7 0.7 maximum_bitcast_fusion.pace_ref
  1.4 0.0 copy-start.1
  1.4 0.9 %copy-done.1 = bf16[1,64,1024]{2,1,0:T(8,128)(2,1)S(1)} copy-done((bf16[1,64,1024]{2,1,0:T(8,128)(2,1)S(1)}, bf16[1,64,1024]{2,1,0:T(8,128)(2,1)}, u32[]{:S(2)}) %copy-start.1) | copy-done | bytes 131096
  2.3 0.3 shard_map.64
  2.6 21.0 %all_to_all.20.rows_ref = bf16[8,64,256]{2,1,0:T(8,128)(2,1)S(1)} all-to-all(bf16[8,64,256]{2,1,0:T(8,128)(2,1)S(1)} %shard_map.64), channel_id=1, replica_groups=mesh['y'=8,'xc'=8,'chan'=8] {'chan'}, dimensions={0} | all-to-all | bytes 524288 | tf_op jit(solution)/shard_map/all_to_all | solution.py:197
  23.6 0.0 copy-start
  23.6 1.7 %copy-done = bf16[9,256,512]{2,1,0:T(8,128)(2,1)S(1)} copy-done((bf16[9,256,512]{2,1,0:T(8,128)(2,1)S(1)}, bf16[9,256,512]{2,1,0:T(8,128)(2,1)}, u32[]{:S(2)}) %copy-start) | copy-done | bytes 2359320
  25.3 0.0 copy-start.2
  25.3 0.0 copy-start.3
  25.3 0.0 copy-start.4
  25.3 0.9 %shard_map.65 = bf16[8,32,256]{2,1,0:T(8,128)(2,1)S(1)} custom-call(f32[1,33]{1,0:T(1,128)S(1)} %maximum_bitcast_fusion.pace_ref, bf16[8,64,256]{2,1,0:T(8,128)(2,1)S(1)} %all_to_all.20.rows_ref, bf16[9,256,512]{2,1,0:T(8,128)(2,1)S(1)} %copy-done), custom_call_target="tpu_custom_call" | custom-call | tf_op jit(solution)/shard_map/pallas_call | solution.py:53
  26.2 11.8 %all_to_all.21.driven_ref = bf16[8,32,256]{2,1,0:T(8,128)(2,1)S(1)} all-to-all(bf16[8,32,256]{2,1,0:T(8,128)(2,1)S(1)} %shard_map.65), channel_id=1, replica_groups=mesh['y'=8,'xc'=8,'chan'=8] {'xc'}, dimensions={0} | all-to-all | bytes 262144 | tf_op jit(solution)/shard_map/all_to_all | solution.py:199
  38.0 0.1 shard_map.66
  38.1 14.5 %all_to_all.22.final_ref = bf16[8,32,256]{2,1,0:T(8,128)(2,1)S(1)} all-to-all(bf16[8,32,256]{2,1,0:T(8,128)(2,1)S(1)} %shard_map.66), channel_id=1, replica_groups=mesh['y'=8,'xc'=8,'chan'=8] {'y'}, dimensions={0} | all-to-all | bytes 262144 | tf_op jit(solution)/shard_map/all_to_all | solution.py:201
  52.6 0.1 shard_map.67
  52.8 22.8 %all_to_all.23 = bf16[64,32,128]{2,1,0:T(8,128)(2,1)S(1)} all-to-all(bf16[64,32,128]{2,1,0:T(8,128)(2,1)S(1)} %bitcast.7), channel_id=1, replica_groups=mesh['y'=8,'xc'=8,'chan'=8] {'xc','chan'}, dimensions={0} | all-to-all | bytes 1048576 | tf_op jit(solution)/shard_map/all_to_all | solution.py:204
  75.6 0.0 copy-done.2
  75.6 0.0 copy-done.3
  75.6 0.0 copy-done.4
  75.6 1.8 %shard_map.68 = bf16[64,1024]{1,0:T(8,128)(2,1)} custom-call(bf16[8,8,32,128]{3,2,1,0:T(8,128)(2,1)S(1)} %bitcast.8, bf16[64,1024]{1,0:T(8,128)(2,1)S(1)} %bitcast.10, bf16[9,64,256]{2,1,0:T(8,128)(2,1)S(1)} %copy-done.3, f32[1,64]{1,0:T(1,128)S(1)} %bitcast.11), custom_call_target="tpu_custom_call" | custom-call | tf_op jit(solution)/shard_map/pallas_call | solution.py:53
Async XLA Ops:
  1.4 0.9 %copy-start.1 = (bf16[1,64,1024]{2,1,0:T(8,128)(2,1)S(1)}, bf16[1,64,1024]{2,1,0:T(8,128)(2,1)}, u32[]{:S(2)}) copy-start(bf16[1,64,1024]{2,1,0:T(8,128)(2,1)} %param.6) | copy-start | bytes 393220
  23.6 1.7 %copy-start = (bf16[9,256,512]{2,1,0:T(8,128)(2,1)S(1)}, bf16[9,256,512]{2,1,0:T(8,128)(2,1)}, u32[]{:S(2)}) copy-start(bf16[9,256,512]{2,1,0:T(8,128)(2,1)} %weight_ref.2) | copy-start | bytes 7077892
  25.3 50.3 %copy-start.2 = (bf16[1,64,1024]{2,1,0:T(8,128)(2,1)S(1)}, bf16[1,64,1024]{2,1,0:T(8,128)(2,1)}, u32[]{:S(2)}) copy-start(bf16[1,64,1024]{2,1,0:T(8,128)(2,1)} %param.6) | copy-start | bytes 393220
  25.3 50.3 %copy-start.3 = (bf16[9,64,256]{2,1,0:T(8,128)(2,1)S(1)}, bf16[9,64,256]{2,1,0:T(8,128)(2,1)}, u32[]{:S(2)}) copy-start(bf16[9,64,256]{2,1,0:T(8,128)(2,1)} %weight_ref.3) | copy-start | bytes 884740
  25.3 50.3 %copy-start.4 = (f32[64]{0:T(128)S(1)}, f32[64]{0:T(128)}, u32[]{:S(2)}) copy-start(f32[64]{0:T(128)} %param.11) | copy-start | bytes 772

commit v4 on v3

--- a/solution.py
+++ b/solution.py
@@ -48,41 +48,68 @@
     return jnp.sum(jnp.where(inside, tile.astype(F32), 0.0), axis=-1, keepdims=True)
 
 
-def call(kernel, outs, *operands, vmem=32):
-    here = pl.BlockSpec(memory_space=pltpu.VMEM)
+def call(kernel, outs, *operands, places=None, scratch=(), vmem=32, cost=None):
+    places = places or (pltpu.VMEM,) * len(operands)
+    specs = [pl.BlockSpec(memory_space=place) for place in places]
     return pl.pallas_call(
         kernel,
         out_shape=outs,
-        in_specs=[here] * len(operands),
-        out_specs=here,
+        in_specs=specs,
+        out_specs=pl.BlockSpec(memory_space=pltpu.VMEM),
+        scratch_shapes=scratch,
+        cost_estimate=cost,
         compiler_params=pltpu.CompilerParams(vmem_limit_bytes=vmem << 20),
     )(*operands)
 
 
-def cut_rows(frame_ref, pace_ref, out_ref):
+def cut_rows(frame_hbm, rate_hbm, out_ref, frame_ref, rate_ref, sems):
+    copies = [
+        pltpu.make_async_copy(source, target, sems.at[n])
+        for n, (source, target) in enumerate([(frame_hbm, frame_ref), (rate_hbm, rate_ref)])
+    ]
+    for copy in copies:
+        copy.start()
+    for copy in copies:
+        copy.wait()
     blocks = out_ref.shape[0]
-    channels = out_ref.shape[1]
+    channels = frame_ref.shape[0]
+    half = channels // 2
     lane = lanes_of((channels, TILE))
-    own = to_column(pace_ref[:, 1:])
-    column = jnp.concatenate([own, jnp.zeros((channels - own.shape[0], 1), F32)], axis=0)
-    meta = spread(column, ROW, (channels, TILE))
+    after_at, before_at = lane < ROW, lane >= TILE - ROW
+    near = lane[:half]
+    outer = (near < ROW) | (near >= TILE - ROW)
+    rate = to_column(rate_ref[...])
+    part = rate.shape[0] // 2
+    meta = spread(rate[:part], 0, (part, TILE)) + spread(rate[part:], 3, (part, TILE))
+    meta = meta.astype(BF)
     for b in range(blocks):
-        out_ref[b, :, :TILE] = frame_ref[:, b * TILE : (b + 1) * TILE]
-        side = meta
+        out_ref[b, :channels] = frame_ref[:, b * TILE : (b + 1) * TILE]
+        side = jnp.zeros((channels, TILE), F32)
         if b + 1 < blocks:
             after = frame_ref[:, (b + 1) * TILE : (b + 2) * TILE].astype(F32)
-            side = jnp.where(lane < ROW, after, side)
+            side = jnp.where(after_at, after, side)
         if b > 0:
             before = frame_ref[:, (b - 1) * TILE : b * TILE].astype(F32)
-            side = jnp.where(lane >= TILE - ROW, before, side)
-        out_ref[b, :, TILE:] = side.astype(BF)
-
-
-def drive(pace_ref, rows_ref, weight_ref, out_ref):
-    blocks, channels, _ = rows_ref.shape
-    states = weight_ref.shape[1]
-    main = rows_ref[:, :, :TILE].reshape(blocks * channels, TILE)
-    side = rows_ref[:, :, TILE:].reshape(blocks * channels, TILE)
+            side = jnp.where(before_at, before, side)
+        packed = jnp.where(outer, side[:half], roll_lanes(side[half:], TILE // 2))
+        out_ref[b, channels : channels + half] = packed.astype(BF)
+        out_ref[b, channels + half :] = meta
+
+
+def drive(step_ref, rows_ref, weight_ref, out_ref):
+    blocks, height, _ = rows_ref.shape
+    states, depth = weight_ref.shape[1:]
+    channels = depth // blocks
+    half = channels // 2
+    main = rows_ref[:, :channels].reshape(depth, TILE)
+    sides = []
+    rates = []
+    for b in range(blocks):
+        packed = rows_ref[b, channels : channels + half]
+        sides += [packed, roll_lanes(packed.astype(F32), TILE // 2).astype(BF)]
+        meta = rows_ref[b, channels + half :]
+        rates += [collect(meta, 0), collect(meta, 3)]
+    side = jnp.concatenate(sides, axis=0)
     lane = lanes_of(main.shape)
     column = lanes_of((states, TILE)) % ROW
     total = None
@@ -93,16 +120,13 @@
             source = jnp.where(lane < ROW, side, main)
         else:
             source = main
-        row = jnp.dot(weight_ref[3 * i + 1], source, preferred_element_type=F32)
-        left = jnp.dot(weight_ref[3 * i], source, preferred_element_type=F32)
-        right = jnp.dot(weight_ref[3 * i + 2], source, preferred_element_type=F32)
+        weight = weight_ref[3 * i : 3 * i + 3].reshape(3 * states, depth)
+        left, row, right = jnp.split(jnp.dot(weight, source, preferred_element_type=F32), 3)
         row = row + jnp.where(column > 0, roll_lanes(left, 1), 0.0)
         row = row + jnp.where(column < ROW - 1, roll_lanes(right, -1), 0.0)
         row = roll_lanes(row, (1 - i) * ROW) if i != 1 else row
         total = row if total is None else total + row
-    own = states // blocks
-    rate = jnp.concatenate([collect(rows_ref[b, :own, TILE:], ROW) for b in range(blocks)], axis=0)
-    decay = jnp.exp(-rate * pace_ref[:, :1])
+    decay = jnp.exp(-jnp.concatenate(rates, axis=0) * step_ref[0])
     inject = jnp.sqrt(1.0 - decay * decay)
     scaled = (inject * total).astype(BF)
     meta = spread(decay, 0, (states, TILE)).astype(BF)
@@ -149,39 +173,33 @@
 def finish(state_ref, frame_ref, weight_ref, gain_ref, out_ref):
     groups, blocks, part, _ = state_ref.shape
     states = groups * part
-    channels, cells = frame_ref.shape
-    tiles = [state_ref[:, b].reshape(states, TILE) for b in range(blocks)]
-    lane = lanes_of((states, TILE))
-    column = lanes_of((channels, cells)) % ROW
-    total = None
-    for i in range(3):
-        if i == 1:
-            source = jnp.concatenate(tiles, axis=1)
-        else:
-            parts = []
-            for b in range(blocks):
-                other = b + i - 1
-                inside = 0 <= other < blocks
-                beside = tiles[other] if inside else jnp.zeros_like(tiles[b])
-                edge = lane < ROW if i == 2 else lane >= TILE - ROW
-                parts.append(jnp.where(edge, beside, tiles[b]))
-            source = jnp.concatenate(parts, axis=1)
-        left = jnp.dot(weight_ref[3 * i], source, preferred_element_type=F32)
-        row = jnp.dot(weight_ref[3 * i + 1], source, preferred_element_type=F32)
-        right = jnp.dot(weight_ref[3 * i + 2], source, preferred_element_type=F32)
-        row = row + jnp.where(column > 0, roll_lanes(left, 1), 0.0)
-        row = row + jnp.where(column < ROW - 1, roll_lanes(right, -1), 0.0)
-        if i != 1:
-            row = jnp.concatenate(
-                [
-                    roll_lanes(row[:, b * TILE : (b + 1) * TILE], (1 - i) * ROW)
-                    for b in range(blocks)
-                ],
-                axis=1,
-            )
-        total = row if total is None else total + row
-    total = total + to_column(gain_ref[...]) * frame_ref[...].astype(F32)
-    out_ref[...] = jax.nn.gelu(total).astype(BF)
+    channels = frame_ref.shape[0]
+    source = jnp.concatenate([state_ref[:, b].reshape(states, TILE) for b in range(blocks)], axis=1)
+    weight = weight_ref[...].reshape(9 * channels, states)
+    taps = jnp.dot(weight, source, preferred_element_type=F32)
+    lane = lanes_of((channels, TILE))
+    column = lane % ROW
+    gain = to_column(gain_ref[...])
+
+    def row(i, b):
+        def tap(j):
+            at = (3 * i + j) * channels
+            return taps[at : at + channels, b * TILE : (b + 1) * TILE]
+
+        left = jnp.where(column > 0, roll_lanes(tap(0), 1), 0.0)
+        right = jnp.where(column < ROW - 1, roll_lanes(tap(2), -1), 0.0)
+        return tap(1) + left + right
+
+    down = [roll_lanes(row(0, b), ROW) for b in range(blocks)]
+    up = [roll_lanes(row(2, b), -ROW) for b in range(blocks)]
+    for b in range(blocks):
+        at = slice(b * TILE, (b + 1) * TILE)
+        before = down[b - 1] if b > 0 else 0.0
+        after = up[b + 1] if b + 1 < blocks else 0.0
+        total = row(1, b) + gain * frame_ref[:, at].astype(F32)
+        total = total + jnp.where(lane < ROW, before, down[b])
+        total = total + jnp.where(lane >= TILE - ROW, after, up[b])
+        out_ref[:, at] = jax.nn.gelu(total).astype(BF)
 
 
 def body(groups, frames, decay_rate, step_size, in_kernel, out_kernel, skip_gain):
@@ -192,10 +210,30 @@
     part = states // members
     frame = frames.reshape(channels, cells)
     shape = jax.ShapeDtypeStruct
-    pace = jnp.concatenate([step_size, decay_rate])[None]
-    cut = call(cut_rows, shape((blocks, channels, 2 * TILE), BF), frame, pace)
+    rates = decay_rate.shape[0]
+    cut = call(
+        cut_rows,
+        shape((blocks, channels + channels // 2 + rates // 2, TILE), BF),
+        frame,
+        decay_rate[None],
+        places=(pltpu.HBM, pltpu.HBM),
+        scratch=(
+            pltpu.VMEM(frame.shape, BF),
+            pltpu.VMEM((1, rates), F32),
+            pltpu.SemaphoreType.DMA((2,)),
+        ),
+        vmem=56,
+        cost=pl.CostEstimate(flops=10**9, bytes_accessed=3 * 10**7, transcendentals=0),
+    )
     rows = lax.all_to_all(cut, "chan", 0, 0, tiled=True)
-    driven = call(drive, shape((members, part, 2 * TILE), BF), pace, rows, in_kernel)
+    driven = call(
+        drive,
+        shape((members, part, 2 * TILE), BF),
+        step_size,
+        rows,
+        in_kernel,
+        places=(pltpu.SMEM, pltpu.VMEM, pltpu.VMEM),
+    )
     driven = lax.all_to_all(driven, "xc", 0, 0, tiled=True)
     final = call(finish_group, shape((groups, part, 2 * TILE), BF), driven)
     final = lax.all_to_all(final, "y", 0, 0, tiled=True)

time: 77.7 us -> 74.7 us (0.961)
  blocking collectives: 70.2 us -> 49.1 us
  starting transfers between devices: 0 us -> 10.9 us
  waiting for transfers between devices: 0 us -> 9.06 us
  local copies, waits for them, and re-layouts: 2.58 us -> 0.02 us
  Pallas kernels: 3.22 us -> 4.6 us
    all_to_all x1 -> x0, blocking collectives: 21 us -> none  [body(): rows = lax.all_to_all(cut, 'chan', 0, 0, tiled=True)]
    all_to_all x0 -> x1, starting transfers between devices: none -> 10.9 us  [body(): rows = lax.all_to_all(cut, 'chan', 0, 0, tiled=True)]
    all_to_all x0 -> x1, waiting for transfers between devices: none -> 9.06 us  [body(): rows = lax.all_to_all(cut, 'chan', 0, 0, tiled=True)]
    unnamed x10 -> x8, local copies, waits for them, and re-layouts: 2.58 us -> 0.02 us
    pallas_call x5, Pallas kernels: 3.22 us -> 4.6 us  [call(): pl.pallas_call(kernel, out_shape=outs, in_specs=specs, out_specs=pl.Block...]
  transfers between devices with their start and end apart: 0 -> 1, of which waited for: 0 -> 1; matrix products, arithmetic and copies ran while one was open for 0% -> 0% of each run, Pallas kernels for 0% -> 0%
where the time goes in v4:
time: 74.7 us; the launch traced here: 74.3 us
  blocking collectives  49.1 us (66%)
  starting transfers between devices  10.9 us (15%)
  waiting for transfers between devices  9.06 us (12%)
  Pallas kernels  4.6 us (6%)
    all_to_all x1, blocking collectives, body(): state = lax.all_to_all(state, ('xc', 'chan'), 0, 0, tiled=True)  22.8 us
    all_to_all x1, blocking collectives, body(): final = lax.all_to_all(final, 'y', 0, 0, tiled=True)  14.5 us
    all_to_all x1, blocking collectives, body(): driven = lax.all_to_all(driven, 'xc', 0, 0, tiled=True)  11.7 us
    all_to_all x1, starting transfers between devices, body(): rows = lax.all_to_all(cut, 'chan', 0, 0, tiled=True)  10.9 us
    all_to_all x1, waiting for transfers between devices, body(): rows = lax.all_to_all(cut, 'chan', 0, 0, tiled=True)  9.06 us
    pallas_call x5, Pallas kernels, call(): pl.pallas_call(kernel, out_shape=outs, in_specs=specs, out_specs=pl.Block...  4.6 us
  transfers between devices with their start and end apart: 1, of which 1 were waited for; matrix products, arithmetic and copies ran while one was open for 0% of the time, Pallas kernels for 0%

profile of v4, /device:TPU:1, one launch (start us, length us, event | category | flops | bytes accessed | tf_op | source)
XLA Modules:
  0.0 74.3 jit_solution(11604716251129511037)
XLA Ops:
  0.0 0.0 copy-start
  0.0 1.9 %shard_map.64 = bf16[8,112,128]{2,1,0:T(8,128)(2,1)} custom-call(bf16[64,1024]{1,0:T(8,128)(2,1)} %bitcast.8, f32[1,32]{1,0:T(1,128)} %bitcast.11), custom_call_target="tpu_custom_call" | custom-call | flops 1000000000 | bytes 30000000 | tf_op jit(solution)/shard_map/pallas_call | solution.py:54
  1.9 10.9 %all-to-all-start = ((bf16[8,112,128]{2,1,0:T(8,128)(2,1)}), bf16[8,112,128]{2,1,0:T(8,128)(2,1)S(1)}, u32[]{:S(2)}, u32[]{:S(2)}) async-start(bf16[8,112,128]{2,1,0:T(8,128)(2,1)} %shard_map.64), calls=%async_computation | async-start | bytes 458752 | tf_op jit(solution)/shard_map/all_to_all | solution.py:228
  13.4 0.0 copy-start.1
  13.4 0.0 copy-start.2
  13.4 0.0 copy-start.3
  13.4 9.1 %all-to-all-done.rows_ref = bf16[8,112,128]{2,1,0:T(8,128)(2,1)S(1)} async-done(((bf16[8,112,128]{2,1,0:T(8,128)(2,1)}), bf16[8,112,128]{2,1,0:T(8,128)(2,1)S(1)}, u32[]{:S(2)}, u32[]{:S(2)}) %all-to-all-start) | async-done | bytes 229408 | tf_op jit(solution)/shard_map/all_to_all | solution.py:228
  22.5 0.0 copy-done
  22.5 1.0 %shard_map.65 = bf16[8,32,256]{2,1,0:T(8,128)(2,1)S(1)} custom-call(f32[1]{0:T(128)S(6)} %copy.7.step_ref, bf16[8,112,128]{2,1,0:T(8,128)(2,1)S(1)} %all-to-all-done.rows_ref, bf16[9,256,512]{2,1,0:T(8,128)(2,1)S(1)} %copy-done), custom_call_target="tpu_custom_call" | custom-call | tf_op jit(solution)/shard_map/pallas_call | solution.py:54
  23.5 11.7 %all_to_all.20.driven_ref = bf16[8,32,256]{2,1,0:T(8,128)(2,1)S(1)} all-to-all(bf16[8,32,256]{2,1,0:T(8,128)(2,1)S(1)} %shard_map.65), channel_id=1, replica_groups=mesh['y'=8,'xc'=8,'chan'=8] {'xc'}, dimensions={0} | all-to-all | bytes 262144 | tf_op jit(solution)/shard_map/all_to_all | solution.py:237
  35.3 0.1 shard_map.66
  35.4 14.5 %all_to_all.21.final_ref = bf16[8,32,256]{2,1,0:T(8,128)(2,1)S(1)} all-to-all(bf16[8,32,256]{2,1,0:T(8,128)(2,1)S(1)} %shard_map.66), channel_id=1, replica_groups=mesh['y'=8,'xc'=8,'chan'=8] {'y'}, dimensions={0} | all-to-all | bytes 262144 | tf_op jit(solution)/shard_map/all_to_all | solution.py:239
  49.9 0.1 shard_map.67
  50.0 22.8 %all_to_all.22 = bf16[64,32,128]{2,1,0:T(8,128)(2,1)S(1)} all-to-all(bf16[64,32,128]{2,1,0:T(8,128)(2,1)S(1)} %bitcast.6), channel_id=1, replica_groups=mesh['y'=8,'xc'=8,'chan'=8] {'xc','chan'}, dimensions={0} | all-to-all | bytes 1048576 | tf_op jit(solution)/shard_map/all_to_all | solution.py:242
  72.8 0.0 copy-done.1
  72.8 0.0 copy-done.2
  72.8 0.0 copy-done.3
  72.9 1.5 %shard_map.68 = bf16[64,1024]{1,0:T(8,128)(2,1)} custom-call(bf16[8,8,32,128]{3,2,1,0:T(8,128)(2,1)S(1)} %bitcast.7, bf16[64,1024]{1,0:T(8,128)(2,1)S(1)} %bitcast.9, bf16[9,64,256]{2,1,0:T(8,128)(2,1)S(1)} %copy-done.1, f32[1,64]{1,0:T(1,128)S(1)} %bitcast.10), custom_call_target="tpu_custom_call" | custom-call | tf_op jit(solution)/shard_map/pallas_call | solution.py:54
Async XLA Ops:
  0.0 22.5 %copy-start = (bf16[9,256,512]{2,1,0:T(8,128)(2,1)S(1)}, bf16[9,256,512]{2,1,0:T(8,128)(2,1)}, u32[]{:S(2)}) copy-start(bf16[9,256,512]{2,1,0:T(8,128)(2,1)} %weight_ref.2) | copy-start | bytes 7077892
  1.9 20.6 %all-to-all-start = ((bf16[8,112,128]{2,1,0:T(8,128)(2,1)}), bf16[8,112,128]{2,1,0:T(8,128)(2,1)S(1)}, u32[]{:S(2)}, u32[]{:S(2)}) async-start(bf16[8,112,128]{2,1,0:T(8,128)(2,1)} %shard_map.64), calls=%async_computation | async-start | bytes 458752 | tf_op jit(solution)/shard_map/all_to_all | solution.py:228
  13.4 59.5 %copy-start.1 = (bf16[9,64,256]{2,1,0:T(8,128)(2,1)S(1)}, bf16[9,64,256]{2,1,0:T(8,128)(2,1)}, u32[]{:S(2)}) copy-start(bf16[9,64,256]{2,1,0:T(8,128)(2,1)} %weight_ref.3) | copy-start | bytes 884740
  13.4 59.4 %copy-start.2 = (bf16[1,64,1024]{2,1,0:T(8,128)(2,1)S(1)}, bf16[1,64,1024]{2,1,0:T(8,128)(2,1)}, u32[]{:S(2)}) copy-start(bf16[1,64,1024]{2,1,0:T(8,128)(2,1)} %param.6) | copy-start | bytes 393220
  13.4 59.4 %copy-start.3 = (f32[64]{0:T(128)S(1)}, f32[64]{0:T(128)}, u32[]{:S(2)}) copy-start(f32[64]{0:T(128)} %param.11) | copy-start | bytes 772

commit v5 on v4

--- a/solution.py
+++ b/solution.py
@@ -62,15 +62,11 @@
     )(*operands)
 
 
-def cut_rows(frame_hbm, rate_hbm, out_ref, frame_ref, rate_ref, sems):
-    copies = [
-        pltpu.make_async_copy(source, target, sems.at[n])
-        for n, (source, target) in enumerate([(frame_hbm, frame_ref), (rate_hbm, rate_ref)])
-    ]
-    for copy in copies:
-        copy.start()
-    for copy in copies:
-        copy.wait()
+def lay_step(step_ref, out_ref):
+    out_ref[...] = jnp.full(out_ref.shape, step_ref[0], F32)
+
+
+def cut_rows(step_ref, frame_ref, rate_ref, out_ref):
     blocks = out_ref.shape[0]
     channels = frame_ref.shape[0]
     half = channels // 2
@@ -80,8 +76,9 @@
     outer = (near < ROW) | (near >= TILE - ROW)
     rate = to_column(rate_ref[...])
     part = rate.shape[0] // 2
-    meta = spread(rate[:part], 0, (part, TILE)) + spread(rate[part:], 3, (part, TILE))
-    meta = meta.astype(BF)
+    tile = (part, TILE)
+    meta = spread(rate[:part], 0, tile) + spread(rate[part:], 3, tile)
+    meta = (meta + spread(jnp.broadcast_to(step_ref[:1, :1], (part, 1)), 6, tile)).astype(BF)
     for b in range(blocks):
         out_ref[b, :channels] = frame_ref[:, b * TILE : (b + 1) * TILE]
         side = jnp.zeros((channels, TILE), F32)
@@ -96,7 +93,7 @@
         out_ref[b, channels + half :] = meta
 
 
-def drive(step_ref, rows_ref, weight_ref, out_ref):
+def drive(rows_ref, weight_ref, out_ref):
     blocks, height, _ = rows_ref.shape
     states, depth = weight_ref.shape[1:]
     channels = depth // blocks
@@ -110,6 +107,7 @@
         meta = rows_ref[b, channels + half :]
         rates += [collect(meta, 0), collect(meta, 3)]
     side = jnp.concatenate(sides, axis=0)
+    step = collect(rows_ref[0, channels + half : channels + half + 8], 6)[:1]
     lane = lanes_of(main.shape)
     column = lanes_of((states, TILE)) % ROW
     total = None
@@ -126,7 +124,7 @@
         row = row + jnp.where(column < ROW - 1, roll_lanes(right, -1), 0.0)
         row = roll_lanes(row, (1 - i) * ROW) if i != 1 else row
         total = row if total is None else total + row
-    decay = jnp.exp(-jnp.concatenate(rates, axis=0) * step_ref[0])
+    decay = jnp.exp(-jnp.concatenate(rates, axis=0) * step)
     inject = jnp.sqrt(1.0 - decay * decay)
     scaled = (inject * total).astype(BF)
     meta = spread(decay, 0, (states, TILE)).astype(BF)
@@ -211,28 +209,27 @@
     frame = frames.reshape(channels, cells)
     shape = jax.ShapeDtypeStruct
     rates = decay_rate.shape[0]
+    step = call(
+        lay_step,
+        shape((8, TILE), F32),
+        step_size,
+        places=(pltpu.SMEM,),
+        cost=pl.CostEstimate(flops=10**9, bytes_accessed=0, transcendentals=0),
+    )
     cut = call(
         cut_rows,
         shape((blocks, channels + channels // 2 + rates // 2, TILE), BF),
+        step,
         frame,
         decay_rate[None],
-        places=(pltpu.HBM, pltpu.HBM),
-        scratch=(
-            pltpu.VMEM(frame.shape, BF),
-            pltpu.VMEM((1, rates), F32),
-            pltpu.SemaphoreType.DMA((2,)),
-        ),
-        vmem=56,
-        cost=pl.CostEstimate(flops=10**9, bytes_accessed=3 * 10**7, transcendentals=0),
+        cost=pl.CostEstimate(flops=10**9, bytes_accessed=0, transcendentals=0),
     )
     rows = lax.all_to_all(cut, "chan", 0, 0, tiled=True)
     driven = call(
         drive,
         shape((members, part, 2 * TILE), BF),
-        step_size,
         rows,
         in_kernel,
-        places=(pltpu.SMEM, pltpu.VMEM, pltpu.VMEM),
     )
     driven = lax.all_to_all(driven, "xc", 0, 0, tiled=True)
     final = call(finish_group, shape((groups, part, 2 * TILE), BF), driven)

time: 74.7 us -> 73.7 us (0.987)
  blocking collectives: 49.1 us -> 69.6 us
  starting transfers between devices: 10.9 us -> 0 us
  waiting for transfers between devices: 9.06 us -> 0 us
  Pallas kernels: 4.6 us -> 2.88 us
    all_to_all x0 -> x1, blocking collectives: none -> 20.5 us  [body(): rows = lax.all_to_all(cut, 'chan', 0, 0, tiled=True)]
    all_to_all x1 -> x0, starting transfers between devices: 10.9 us -> none  [body(): rows = lax.all_to_all(cut, 'chan', 0, 0, tiled=True)]
    all_to_all x1 -> x0, waiting for transfers between devices: 9.06 us -> none  [body(): rows = lax.all_to_all(cut, 'chan', 0, 0, tiled=True)]
    pallas_call x5 -> x6, Pallas kernels: 4.6 us -> 2.88 us  [call(): pl.pallas_call(kernel, out_shape=outs, in_specs=specs, out_specs=pl.Block...]
  transfers between devices with their start and end apart: 1 -> 0, of which waited for: 1 -> 0; matrix products, arithmetic and copies ran while one was open for 0% -> 0% of each run, Pallas kernels for 0% -> 0%
where the time goes in v5:
time: 73.7 us; the launch traced here: 73.5 us
  blocking collectives  69.6 us (94%)
  Pallas kernels  2.88 us (4%)
  between operations  0.75 us (1%)
    all_to_all x1, blocking collectives, body(): state = lax.all_to_all(state, ('xc', 'chan'), 0, 0, tiled=True)  22.8 us
    all_to_all x1, blocking collectives, body(): rows = lax.all_to_all(cut, 'chan', 0, 0, tiled=True)  20.5 us
    all_to_all x1, blocking collectives, body(): final = lax.all_to_all(final, 'y', 0, 0, tiled=True)  14.5 us
    all_to_all x1, blocking collectives, body(): driven = lax.all_to_all(driven, 'xc', 0, 0, tiled=True)  11.7 us
    pallas_call x6, Pallas kernels, call(): pl.pallas_call(kernel, out_shape=outs, in_specs=specs, out_specs=pl.Block...  2.88 us

profile of v5, /device:TPU:1, one launch (start us, length us, event | category | flops | bytes accessed | tf_op | source)
XLA Modules:
  0.0 73.5 jit_solution(14076484655620403443)
XLA Ops:
  0.0 0.0 copy-start.4
  0.0 0.0 copy-start.2
  0.7 0.0 copy-start
  0.7 0.0 copy-done.4
  0.7 0.2 copy-done.2
  0.9 0.1 shard_map.65
  1.1 20.5 %all_to_all.20.rows_ref = bf16[8,112,128]{2,1,0:T(8,128)(2,1)S(1)} all-to-all(bf16[8,112,128]{2,1,0:T(8,128)(2,1)S(1)} %shard_map.65), channel_id=1, replica_groups=mesh['y'=8,'xc'=8,'chan'=8] {'chan'}, dimensions={0} | all-to-all | bytes 458752 | tf_op jit(solution)/shard_map/all_to_all | solution.py:227
  21.6 0.0 copy-done
  21.6 0.0 copy-start.1
  21.6 0.0 copy-start.3
  21.6 1.0 %shard_map.66 = bf16[8,32,256]{2,1,0:T(8,128)(2,1)S(1)} custom-call(bf16[8,112,128]{2,1,0:T(8,128)(2,1)S(1)} %all_to_all.20.rows_ref, bf16[9,256,512]{2,1,0:T(8,128)(2,1)S(1)} %copy-done), custom_call_target="tpu_custom_call" | custom-call | tf_op jit(solution)/shard_map/pallas_call | solution.py:54
  22.6 11.7 %all_to_all.21.driven_ref = bf16[8,32,256]{2,1,0:T(8,128)(2,1)S(1)} all-to-all(bf16[8,32,256]{2,1,0:T(8,128)(2,1)S(1)} %shard_map.66), channel_id=1, replica_groups=mesh['y'=8,'xc'=8,'chan'=8] {'xc'}, dimensions={0} | all-to-all | bytes 262144 | tf_op jit(solution)/shard_map/all_to_all | solution.py:234
  34.4 0.1 shard_map.67
  34.5 14.5 %all_to_all.22.final_ref = bf16[8,32,256]{2,1,0:T(8,128)(2,1)S(1)} all-to-all(bf16[8,32,256]{2,1,0:T(8,128)(2,1)S(1)} %shard_map.67), channel_id=1, replica_groups=mesh['y'=8,'xc'=8,'chan'=8] {'y'}, dimensions={0} | all-to-all | bytes 262144 | tf_op jit(solution)/shard_map/all_to_all | solution.py:236
  49.0 0.1 shard_map.68
  49.1 22.8 %all_to_all.23 = bf16[64,32,128]{2,1,0:T(8,128)(2,1)S(1)} all-to-all(bf16[64,32,128]{2,1,0:T(8,128)(2,1)S(1)} %bitcast.6), channel_id=1, replica_groups=mesh['y'=8,'xc'=8,'chan'=8] {'xc','chan'}, dimensions={0} | all-to-all | bytes 1048576 | tf_op jit(solution)/shard_map/all_to_all | solution.py:239
  72.0 0.0 copy-done.1
  72.0 0.0 copy-done.3
  72.0 1.5 %shard_map.69 = bf16[64,1024]{1,0:T(8,128)(2,1)} custom-call(bf16[8,8,32,128]{3,2,1,0:T(8,128)(2,1)S(1)} %bitcast.7, bf16[64,1024]{1,0:T(8,128)(2,1)S(1)} %bitcast.9, bf16[9,64,256]{2,1,0:T(8,128)(2,1)S(1)} %copy-done.1, f32[1,64]{1,0:T(1,128)S(1)} %bitcast.10), custom_call_target="tpu_custom_call" | custom-call | tf_op jit(solution)/shard_map/pallas_call | solution.py:54
  (1 shorter events, 0.0 us)
Async XLA Ops:
  0.0 0.7 copy-start.4
  0.0 0.9 %copy-start.2 = (bf16[1,64,1024]{2,1,0:T(8,128)(2,1)S(1)}, bf16[1,64,1024]{2,1,0:T(8,128)(2,1)}, u32[]{:S(2)}) copy-start(bf16[1,64,1024]{2,1,0:T(8,128)(2,1)} %param.6) | copy-start | bytes 393220
  0.7 20.9 %copy-start = (bf16[9,256,512]{2,1,0:T(8,128)(2,1)S(1)}, bf16[9,256,512]{2,1,0:T(8,128)(2,1)}, u32[]{:S(2)}) copy-start(bf16[9,256,512]{2,1,0:T(8,128)(2,1)} %weight_ref.2) | copy-start | bytes 7077892
  21.6 50.4 %copy-start.1 = (bf16[9,64,256]{2,1,0:T(8,128)(2,1)S(1)}, bf16[9,64,256]{2,1,0:T(8,128)(2,1)}, u32[]{:S(2)}) copy-start(bf16[9,64,256]{2,1,0:T(8,128)(2,1)} %weight_ref.3) | copy-start | bytes 884740
  21.6 50.4 %copy-start.3 = (f32[64]{0:T(128)S(1)}, f32[64]{0:T(128)}, u32[]{:S(2)}) copy-start(f32[64]{0:T(128)} %param.11) | copy-start | bytes 772

commit v6 on v5

--- a/solution.py
+++ b/solution.py
@@ -66,7 +66,7 @@
     out_ref[...] = jnp.full(out_ref.shape, step_ref[0], F32)
 
 
-def cut_rows(step_ref, frame_ref, rate_ref, out_ref):
+def cut_rows(order, step_ref, frame_ref, rate_ref, out_ref):
     blocks = out_ref.shape[0]
     channels = frame_ref.shape[0]
     half = channels // 2
@@ -79,8 +79,8 @@
     tile = (part, TILE)
     meta = spread(rate[:part], 0, tile) + spread(rate[part:], 3, tile)
     meta = (meta + spread(jnp.broadcast_to(step_ref[:1, :1], (part, 1)), 6, tile)).astype(BF)
-    for b in range(blocks):
-        out_ref[b, :channels] = frame_ref[:, b * TILE : (b + 1) * TILE]
+    for at, b in enumerate(order):
+        out_ref[at, :channels] = frame_ref[:, b * TILE : (b + 1) * TILE]
         side = jnp.zeros((channels, TILE), F32)
         if b + 1 < blocks:
             after = frame_ref[:, (b + 1) * TILE : (b + 2) * TILE].astype(F32)
@@ -89,22 +89,23 @@
             before = frame_ref[:, (b - 1) * TILE : b * TILE].astype(F32)
             side = jnp.where(before_at, before, side)
         packed = jnp.where(outer, side[:half], roll_lanes(side[half:], TILE // 2))
-        out_ref[b, channels : channels + half] = packed.astype(BF)
-        out_ref[b, channels + half :] = meta
-
-
-def drive(rows_ref, weight_ref, out_ref):
+        out_ref[at, channels : channels + half] = packed.astype(BF)
+        out_ref[at, channels + half :] = meta
+
+
+def drive(order, part_order, rows_ref, weight_ref, out_ref):
     blocks, height, _ = rows_ref.shape
     states, depth = weight_ref.shape[1:]
     channels = depth // blocks
     half = channels // 2
-    main = rows_ref[:, :channels].reshape(depth, TILE)
+    main = jnp.concatenate([rows_ref[order.index(b), :channels] for b in range(blocks)], axis=0)
     sides = []
     rates = []
     for b in range(blocks):
-        packed = rows_ref[b, channels : channels + half]
+        at = order.index(b)
+        packed = rows_ref[at, channels : channels + half]
         sides += [packed, roll_lanes(packed.astype(F32), TILE // 2).astype(BF)]
-        meta = rows_ref[b, channels + half :]
+        meta = rows_ref[at, channels + half :]
         rates += [collect(meta, 0), collect(meta, 3)]
     side = jnp.concatenate(sides, axis=0)
     step = collect(rows_ref[0, channels + half : channels + half + 8], 6)[:1]
@@ -129,18 +130,19 @@
     scaled = (inject * total).astype(BF)
     meta = spread(decay, 0, (states, TILE)).astype(BF)
     group, part, _ = out_ref.shape
-    for g in range(group):
-        out_ref[g, :, :TILE] = scaled[g * part : (g + 1) * part]
-        out_ref[g, :, TILE:] = meta[g * part : (g + 1) * part]
-
-
-def finish_group(driven_ref, out_ref):
+    for at, g in enumerate(part_order):
+        out_ref[at, :, :TILE] = scaled[g * part : (g + 1) * part]
+        out_ref[at, :, TILE:] = meta[g * part : (g + 1) * part]
+
+
+def finish_group(order, driven_ref, out_ref):
     frames, part, _ = driven_ref.shape
     state = None
     through = None
     for f in range(frames):
-        decay = collect(driven_ref[f, :, TILE:], 0)
-        value = driven_ref[f, :, :TILE].astype(F32)
+        at = order.index(f)
+        decay = collect(driven_ref[at, :, TILE:], 0)
+        value = driven_ref[at, :, :TILE].astype(F32)
         state = value if f == 0 else decay * state + value
         through = decay if f == 0 else decay * through
     final = state.astype(BF)
@@ -150,29 +152,36 @@
         out_ref[g, :, TILE:] = meta
 
 
-def run_group(final_ref, driven_ref, out_ref):
+def run_group(order, frame_order, spread_order, final_ref, driven_ref, out_ref):
     groups = final_ref.shape[0]
     frames, part, _ = driven_ref.shape
     at = lax.axis_index("y")
     state = jnp.zeros((part, TILE), F32)
     for g in range(groups):
-        through = collect(final_ref[g, :, TILE:], 0)
-        moved = through * state + final_ref[g, :, :TILE].astype(F32)
+        source = order.index(g)
+        through = collect(final_ref[source, :, TILE:], 0)
+        moved = through * state + final_ref[source, :, :TILE].astype(F32)
         state = jnp.where(g < at, moved, state)
-    copies = out_ref.shape[1]
+    copies = out_ref.shape[0] // frames
     for f in range(frames):
-        decay = collect(driven_ref[f, :, TILE:], 0)
-        state = decay * state + driven_ref[f, :, :TILE].astype(F32)
+        source = frame_order.index(f)
+        decay = collect(driven_ref[source, :, TILE:], 0)
+        state = decay * state + driven_ref[source, :, :TILE].astype(F32)
         rounded = state.astype(BF)
         for c in range(copies):
-            out_ref[f, c] = rounded
-
-
-def finish(state_ref, frame_ref, weight_ref, gain_ref, out_ref):
-    groups, blocks, part, _ = state_ref.shape
-    states = groups * part
-    channels = frame_ref.shape[0]
-    source = jnp.concatenate([state_ref[:, b].reshape(states, TILE) for b in range(blocks)], axis=1)
+            out_ref[spread_order.index(f * copies + c)] = rounded
+
+
+def finish(order, state_ref, frame_ref, weight_ref, gain_ref, out_ref):
+    channels, cells = frame_ref.shape
+    blocks = cells // TILE
+    states = weight_ref.shape[2]
+    parts = len(order) // blocks
+
+    def rows(b):
+        return jnp.concatenate([state_ref[order.index(p * blocks + b)] for p in range(parts)], axis=0)
+
+    source = jnp.concatenate([rows(b) for b in range(blocks)], axis=1)
     weight = weight_ref[...].reshape(9 * channels, states)
     taps = jnp.dot(weight, source, preferred_element_type=F32)
     lane = lanes_of((channels, TILE))
@@ -198,6 +207,16 @@
         total = total + jnp.where(lane < ROW, before, down[b])
         total = total + jnp.where(lane >= TILE - ROW, after, up[b])
         out_ref[:, at] = jax.nn.gelu(total).astype(BF)
+
+
+Z_ORDER = [0, 4, 2, 6, 1, 5, 3, 7]
+Y_ORDER = [0, 4, 2, 6, 1, 5, 3, 7]
+X_ORDER = [0, 1, 2, 3, 4, 5, 6, 7]
+S_ORDER = [i * 8 + k for i in [0, 2, 4, 6, 1, 3, 5, 7] for k in Z_ORDER]
+
+
+def exchange(x, axis, order):
+    return lax.all_to_all(x, axis, 0, 0, axis_index_groups=[order], tiled=True)
 
 
 def body(groups, frames, decay_rate, step_size, in_kernel, out_kernel, skip_gain):
@@ -217,28 +236,38 @@
         cost=pl.CostEstimate(flops=10**9, bytes_accessed=0, transcendentals=0),
     )
     cut = call(
-        cut_rows,
+        functools.partial(cut_rows, Z_ORDER),
         shape((blocks, channels + channels // 2 + rates // 2, TILE), BF),
         step,
         frame,
         decay_rate[None],
         cost=pl.CostEstimate(flops=10**9, bytes_accessed=0, transcendentals=0),
     )
-    rows = lax.all_to_all(cut, "chan", 0, 0, tiled=True)
+    rows = exchange(cut, "chan", Z_ORDER)
     driven = call(
-        drive,
+        functools.partial(drive, Z_ORDER, X_ORDER),
         shape((members, part, 2 * TILE), BF),
         rows,
         in_kernel,
     )
-    driven = lax.all_to_all(driven, "xc", 0, 0, tiled=True)
-    final = call(finish_group, shape((groups, part, 2 * TILE), BF), driven)
-    final = lax.all_to_all(final, "y", 0, 0, tiled=True)
-    state = call(run_group, shape((members, blocks, part, TILE), BF), final, driven)
-    state = state.reshape(members * blocks, part, TILE)
-    state = lax.all_to_all(state, ("xc", "chan"), 0, 0, tiled=True)
-    state = state.reshape(members, blocks, part, TILE)
-    out = call(finish, shape((channels, cells), BF), state, frame, out_kernel, skip_gain[None])
+    driven = exchange(driven, "xc", X_ORDER)
+    final = call(functools.partial(finish_group, X_ORDER), shape((groups, part, 2 * TILE), BF), driven)
+    final = exchange(final, "y", Y_ORDER)
+    state = call(
+        functools.partial(run_group, Y_ORDER, X_ORDER, S_ORDER),
+        shape((members * blocks, part, TILE), BF),
+        final,
+        driven,
+    )
+    state = exchange(state, ("xc", "chan"), S_ORDER)
+    out = call(
+        functools.partial(finish, S_ORDER),
+        shape((channels, cells), BF),
+        state,
+        frame,
+        out_kernel,
+        skip_gain[None],
+    )
     return out[None]
 
 

time: 73.7 us -> 71.8 us (0.974)
  blocking collectives: 69.6 us -> 67.7 us
    all_to_all x4, blocking collectives: 69.6 us -> 67.7 us  [exchange(): return lax.all_to_all(x, axis, 0, 0, axis_index_groups=[order], tiled=True)]
where the time goes in v6:
time: 71.8 us; the launch traced here: 71.6 us
  blocking collectives  67.7 us (94%)
  Pallas kernels  2.88 us (4%)
  between operations  0.75 us (1%)
    all_to_all x4, blocking collectives, exchange(): return lax.all_to_all(x, axis, 0, 0, axis_index_groups=[order], tiled=True)  67.7 us
    pallas_call x6, Pallas kernels, call(): pl.pallas_call(kernel, out_shape=outs, in_specs=specs, out_specs=pl.Block...  2.88 us

profile of v6, /device:TPU:1, one launch (start us, length us, event | category | flops | bytes accessed | tf_op | source)
XLA Modules:
  0.0 71.6 jit_solution(17358184591662901017)
XLA Ops:
  0.0 0.0 copy-start.4
  0.0 0.0 copy-start.2
  0.7 0.0 copy-start
  0.7 0.0 copy-done.4
  0.7 0.2 copy-done.2
  0.9 0.1 shard_map.65
  1.1 17.8 %all_to_all.20.rows_ref = bf16[8,112,128]{2,1,0:T(8,128)(2,1)S(1)} all-to-all(bf16[8,112,128]{2,1,0:T(8,128)(2,1)S(1)} %shard_map.65), channel_id=1, replica_groups={{0,4,2,6,1,5,3,7},{8,12,10,14,9,13,11,15},{16,20,18,22,17,21,19,23},{24..., dimensions={0} | all-to-all | bytes 458752 | tf_op jit(solution)/shard_map/all_to_all | solution.py:219
  18.8 0.0 copy-done
  18.8 0.0 copy-start.1
  18.8 0.0 copy-start.3
  18.8 1.0 %shard_map.66 = bf16[8,32,256]{2,1,0:T(8,128)(2,1)S(1)} custom-call(bf16[8,112,128]{2,1,0:T(8,128)(2,1)S(1)} %all_to_all.20.rows_ref, bf16[9,256,512]{2,1,0:T(8,128)(2,1)S(1)} %copy-done), custom_call_target="tpu_custom_call" | custom-call | tf_op jit(solution)/shard_map/pallas_call | solution.py:54
  19.8 12.0 %all_to_all.21.driven_ref = bf16[8,32,256]{2,1,0:T(8,128)(2,1)S(1)} all-to-all(bf16[8,32,256]{2,1,0:T(8,128)(2,1)S(1)} %shard_map.66), channel_id=1, replica_groups={{0,8,16,24,32,40,48,56},{1,9,17,25,33,41,49,57},{2,10,18,26,34,42,50,58..., dimensions={0} | all-to-all | bytes 262144 | tf_op jit(solution)/shard_map/all_to_all | solution.py:219
  31.9 0.1 shard_map.67
  32.0 13.4 %all_to_all.22.final_ref = bf16[8,32,256]{2,1,0:T(8,128)(2,1)S(1)} all-to-all(bf16[8,32,256]{2,1,0:T(8,128)(2,1)S(1)} %shard_map.67), channel_id=1, replica_groups={{0,256,128,384,64,320,192,448},{1,257,129,385,65,321,193,449},{2,258,13..., dimensions={0} | all-to-all | bytes 262144 | tf_op jit(solution)/shard_map/all_to_all | solution.py:219
  45.4 0.1 shard_map.68
  45.6 24.5 %all_to_all.23.state_ref = bf16[64,32,128]{2,1,0:T(8,128)(2,1)S(1)} all-to-all(bf16[64,32,128]{2,1,0:T(8,128)(2,1)S(1)} %shard_map.68), channel_id=1, replica_groups={{0,4,2,6,1,5,3,7,16,20,18,22,17,21,19,23,32,36,34,38,33,37,35,39,48,52,..., dimensions={0} | all-to-all | bytes 1048576 | tf_op jit(solution)/shard_map/all_to_all | solution.py:219
  70.1 0.0 copy-done.1
  70.1 0.0 copy-done.3
  70.1 1.5 %shard_map.69 = bf16[64,1024]{1,0:T(8,128)(2,1)} custom-call(bf16[64,32,128]{2,1,0:T(8,128)(2,1)S(1)} %all_to_all.23.state_ref, bf16[64,1024]{1,0:T(8,128)(2,1)S(1)} %bitcast.5, bf16[9,64,256]{2,1,0:T(8,128)(2,1)S(1)} %copy-done.1, f32[1,64]{1,0:T(1,128)S(1)} %bitcast.6), custom_call_target="tpu_custom_call" | custom-call | tf_op jit(solution)/shard_map/pallas_call | solution.py:54
  (1 shorter events, 0.0 us)
Async XLA Ops:
  0.0 0.7 %copy-start.4 = (f32[32]{0:T(128)S(1)}, f32[32]{0:T(128)}, u32[]{:S(2)}) copy-start(f32[32]{0:T(128)} %param.7) | copy-start | bytes 388
  0.0 0.9 %copy-start.2 = (bf16[1,64,1024]{2,1,0:T(8,128)(2,1)S(1)}, bf16[1,64,1024]{2,1,0:T(8,128)(2,1)}, u32[]{:S(2)}) copy-start(bf16[1,64,1024]{2,1,0:T(8,128)(2,1)} %param.6) | copy-start | bytes 393220
  0.7 18.1 %copy-start = (bf16[9,256,512]{2,1,0:T(8,128)(2,1)S(1)}, bf16[9,256,512]{2,1,0:T(8,128)(2,1)}, u32[]{:S(2)}) copy-start(bf16[9,256,512]{2,1,0:T(8,128)(2,1)} %weight_ref.2) | copy-start | bytes 7077892
  18.8 51.3 %copy-start.1 = (bf16[9,64,256]{2,1,0:T(8,128)(2,1)S(1)}, bf16[9,64,256]{2,1,0:T(8,128)(2,1)}, u32[]{:S(2)}) copy-start(bf16[9,64,256]{2,1,0:T(8,128)(2,1)} %weight_ref.3) | copy-start | bytes 884740
  18.8 51.3 %copy-start.3 = (f32[64]{0:T(128)S(1)}, f32[64]{0:T(128)}, u32[]{:S(2)}) copy-start(f32[64]{0:T(128)} %param.11) | copy-start | bytes 772

commit v7 on v6

--- a/solution.py
+++ b/solution.py
@@ -209,10 +209,10 @@
         out_ref[:, at] = jax.nn.gelu(total).astype(BF)
 
 
-Z_ORDER = [0, 4, 2, 6, 1, 5, 3, 7]
-Y_ORDER = [0, 4, 2, 6, 1, 5, 3, 7]
-X_ORDER = [0, 1, 2, 3, 4, 5, 6, 7]
-S_ORDER = [i * 8 + k for i in [0, 2, 4, 6, 1, 3, 5, 7] for k in Z_ORDER]
+Z_ORDER = [5, 1, 7, 3, 4, 2, 6, 0]
+Y_ORDER = [4, 0, 6, 2, 5, 1, 7, 3]
+X_ORDER = [5, 4, 7, 6, 1, 0, 3, 2]
+S_ORDER = [i * 8 + k for i in [5, 7, 0, 2, 4, 6, 1, 3] for k in [4, 2, 6, 1, 5, 3, 7, 0]]
 
 
 def exchange(x, axis, order):

time: 71.8 us -> 67 us (0.933)
  blocking collectives: 67.7 us -> 62.9 us
    all_to_all x4, blocking collectives: 67.7 us -> 62.9 us  [exchange(): return lax.all_to_all(x, axis, 0, 0, axis_index_groups=[order], tiled=True)]
where the time goes in v7:
time: 67 us; the launch traced here: 66.8 us
  blocking collectives  62.9 us (94%)
  Pallas kernels  2.87 us (4%)
  between operations  0.75 us (1%)
    all_to_all x4, blocking collectives, exchange(): return lax.all_to_all(x, axis, 0, 0, axis_index_groups=[order], tiled=True)  62.9 us
    pallas_call x6, Pallas kernels, call(): pl.pallas_call(kernel, out_shape=outs, in_specs=specs, out_specs=pl.Block...  2.87 us

profile of v7, /device:TPU:1, one launch (start us, length us, event | category | flops | bytes accessed | tf_op | source)
XLA Modules:
  0.0 66.8 jit_solution(13717739615900077434)
XLA Ops:
  0.0 0.0 copy-start.4
  0.0 0.0 copy-start.2
  0.7 0.0 copy-start
  0.7 0.0 copy-done.4
  0.7 0.2 copy-done.2
  0.9 0.1 shard_map.65
  1.1 19.6 %all_to_all.20.rows_ref = bf16[8,112,128]{2,1,0:T(8,128)(2,1)S(1)} all-to-all(bf16[8,112,128]{2,1,0:T(8,128)(2,1)S(1)} %shard_map.65), channel_id=1, replica_groups={{5,1,7,3,4,2,6,0},{13,9,15,11,12,10,14,8},{21,17,23,19,20,18,22,16},{29..., dimensions={0} | all-to-all | bytes 458752 | tf_op jit(solution)/shard_map/all_to_all | solution.py:219
  20.6 0.0 copy-done
  20.6 0.0 copy-start.1
  20.6 0.0 copy-start.3
  20.6 1.0 %shard_map.66 = bf16[8,32,256]{2,1,0:T(8,128)(2,1)S(1)} custom-call(bf16[8,112,128]{2,1,0:T(8,128)(2,1)S(1)} %all_to_all.20.rows_ref, bf16[9,256,512]{2,1,0:T(8,128)(2,1)S(1)} %copy-done), custom_call_target="tpu_custom_call" | custom-call | tf_op jit(solution)/shard_map/pallas_call | solution.py:54
  21.7 8.8 %all_to_all.21.driven_ref = bf16[8,32,256]{2,1,0:T(8,128)(2,1)S(1)} all-to-all(bf16[8,32,256]{2,1,0:T(8,128)(2,1)S(1)} %shard_map.66), channel_id=1, replica_groups={{40,32,56,48,8,0,24,16},{41,33,57,49,9,1,25,17},{42,34,58,50,10,2,26,18..., dimensions={0} | all-to-all | bytes 262144 | tf_op jit(solution)/shard_map/all_to_all | solution.py:219
  30.5 0.1 shard_map.67
  30.6 11.8 %all_to_all.22.final_ref = bf16[8,32,256]{2,1,0:T(8,128)(2,1)S(1)} all-to-all(bf16[8,32,256]{2,1,0:T(8,128)(2,1)S(1)} %shard_map.67), channel_id=1, replica_groups={{256,0,384,128,320,64,448,192},{257,1,385,129,321,65,449,193},{258,2,38..., dimensions={0} | all-to-all | bytes 262144 | tf_op jit(solution)/shard_map/all_to_all | solution.py:219
  42.4 0.1 shard_map.68
  42.5 22.8 %all_to_all.23.state_ref = bf16[64,32,128]{2,1,0:T(8,128)(2,1)S(1)} all-to-all(bf16[64,32,128]{2,1,0:T(8,128)(2,1)S(1)} %shard_map.68), channel_id=1, replica_groups={{44,42,46,41,45,43,47,40,60,58,62,57,61,59,63,56,4,2,6,1,5,3,7,0,20,18,..., dimensions={0} | all-to-all | bytes 1048576 | tf_op jit(solution)/shard_map/all_to_all | solution.py:219
  65.3 0.0 copy-done.1
  65.3 0.0 copy-done.3
  65.3 1.5 %shard_map.69 = bf16[64,1024]{1,0:T(8,128)(2,1)} custom-call(bf16[64,32,128]{2,1,0:T(8,128)(2,1)S(1)} %all_to_all.23.state_ref, bf16[64,1024]{1,0:T(8,128)(2,1)S(1)} %bitcast.5, bf16[9,64,256]{2,1,0:T(8,128)(2,1)S(1)} %copy-done.1, f32[1,64]{1,0:T(1,128)S(1)} %bitcast.6), custom_call_target="tpu_custom_call" | custom-call | tf_op jit(solution)/shard_map/pallas_call | solution.py:54
  (1 shorter events, 0.0 us)
Async XLA Ops:
  0.0 0.7 %copy-start.4 = (f32[32]{0:T(128)S(1)}, f32[32]{0:T(128)}, u32[]{:S(2)}) copy-start(f32[32]{0:T(128)} %param.7) | copy-start | bytes 388
  0.0 0.9 %copy-start.2 = (bf16[1,64,1024]{2,1,0:T(8,128)(2,1)S(1)}, bf16[1,64,1024]{2,1,0:T(8,128)(2,1)}, u32[]{:S(2)}) copy-start(bf16[1,64,1024]{2,1,0:T(8,128)(2,1)} %param.6) | copy-start | bytes 393220
  0.7 19.9 %copy-start = (bf16[9,256,512]{2,1,0:T(8,128)(2,1)S(1)}, bf16[9,256,512]{2,1,0:T(8,128)(2,1)}, u32[]{:S(2)}) copy-start(bf16[9,256,512]{2,1,0:T(8,128)(2,1)} %weight_ref.2) | copy-start | bytes 7077892
  20.6 44.7 %copy-start.1 = (bf16[9,64,256]{2,1,0:T(8,128)(2,1)S(1)}, bf16[9,64,256]{2,1,0:T(8,128)(2,1)}, u32[]{:S(2)}) copy-start(bf16[9,64,256]{2,1,0:T(8,128)(2,1)} %weight_ref.3) | copy-start | bytes 884740
  20.6 44.7 %copy-start.3 = (f32[64]{0:T(128)S(1)}, f32[64]{0:T(128)}, u32[]{:S(2)}) copy-start(f32[64]{0:T(128)} %param.11) | copy-start | bytes 772

commit v8 on v7

--- a/solution.py
+++ b/solution.py
@@ -210,9 +210,9 @@
 
 
 Z_ORDER = [5, 1, 7, 3, 4, 2, 6, 0]
-Y_ORDER = [4, 0, 6, 2, 5, 1, 7, 3]
-X_ORDER = [5, 4, 7, 6, 1, 0, 3, 2]
-S_ORDER = [i * 8 + k for i in [5, 7, 0, 2, 4, 6, 1, 3] for k in [4, 2, 6, 1, 5, 3, 7, 0]]
+Y_ORDER = [4, 2, 6, 1, 5, 3, 7, 0]
+X_ORDER = [5, 7, 1, 3, 4, 6, 0, 2]
+S_ORDER = [i * 8 + k for ks in ([4, 6, 5, 3, 7], [2, 1, 0]) for i in [5, 7, 0, 2, 4, 6, 1, 3] for k in ks]
 
 
 def exchange(x, axis, order):

time: 67 us -> 66.9 us (level)
  no operation moved by 1% of the time
where the time goes in v8:
time: 66.9 us; the launch traced here: 66.6 us
  blocking collectives  62.8 us (94%)
  Pallas kernels  2.87 us (4%)
  between operations  0.75 us (1%)
    all_to_all x4, blocking collectives, exchange(): return lax.all_to_all(x, axis, 0, 0, axis_index_groups=[order], tiled=True)  62.8 us
    pallas_call x6, Pallas kernels, call(): pl.pallas_call(kernel, out_shape=outs, in_specs=specs, out_specs=pl.Block...  2.87 us

profile of v8, /device:TPU:1, one launch (start us, length us, event | category | flops | bytes accessed | tf_op | source)
XLA Modules:
  0.0 66.6 jit_solution(9383748879980305719)
XLA Ops:
  0.0 0.0 copy-start.4
  0.0 0.0 copy-start.2
  0.7 0.0 copy-start
  0.7 0.0 copy-done.4
  0.7 0.2 copy-done.2
  0.9 0.1 shard_map.65
  1.1 19.6 %all_to_all.20.rows_ref = bf16[8,112,128]{2,1,0:T(8,128)(2,1)S(1)} all-to-all(bf16[8,112,128]{2,1,0:T(8,128)(2,1)S(1)} %shard_map.65), channel_id=1, replica_groups={{5,1,7,3,4,2,6,0},{13,9,15,11,12,10,14,8},{21,17,23,19,20,18,22,16},{29..., dimensions={0} | all-to-all | bytes 458752 | tf_op jit(solution)/shard_map/all_to_all | solution.py:219
  20.6 0.0 copy-done
  20.6 0.0 copy-start.1
  20.6 0.0 copy-start.3
  20.6 1.0 %shard_map.66 = bf16[8,32,256]{2,1,0:T(8,128)(2,1)S(1)} custom-call(bf16[8,112,128]{2,1,0:T(8,128)(2,1)S(1)} %all_to_all.20.rows_ref, bf16[9,256,512]{2,1,0:T(8,128)(2,1)S(1)} %copy-done), custom_call_target="tpu_custom_call" | custom-call | tf_op jit(solution)/shard_map/pallas_call | solution.py:54
  21.7 8.4 %all_to_all.21.driven_ref = bf16[8,32,256]{2,1,0:T(8,128)(2,1)S(1)} all-to-all(bf16[8,32,256]{2,1,0:T(8,128)(2,1)S(1)} %shard_map.66), channel_id=1, replica_groups={{40,56,8,24,32,48,0,16},{41,57,9,25,33,49,1,17},{42,58,10,26,34,50,2,18..., dimensions={0} | all-to-all | bytes 262144 | tf_op jit(solution)/shard_map/all_to_all | solution.py:219
  30.0 0.1 shard_map.67
  30.2 11.5 %all_to_all.22.final_ref = bf16[8,32,256]{2,1,0:T(8,128)(2,1)S(1)} all-to-all(bf16[8,32,256]{2,1,0:T(8,128)(2,1)S(1)} %shard_map.67), channel_id=1, replica_groups={{256,128,384,64,320,192,448,0},{257,129,385,65,321,193,449,1},{258,130,..., dimensions={0} | all-to-all | bytes 262144 | tf_op jit(solution)/shard_map/all_to_all | solution.py:219
  41.7 0.1 shard_map.68
  41.8 23.3 %all_to_all.23.state_ref = bf16[64,32,128]{2,1,0:T(8,128)(2,1)S(1)} all-to-all(bf16[64,32,128]{2,1,0:T(8,128)(2,1)S(1)} %shard_map.68), channel_id=1, replica_groups={{44,46,45,43,47,60,62,61,59,63,4,6,5,3,7,20,22,21,19,23,36,38,37,35,39,..., dimensions={0} | all-to-all | bytes 1048576 | tf_op jit(solution)/shard_map/all_to_all | solution.py:219
  65.2 0.0 copy-done.1
  65.2 0.0 copy-done.3
  65.2 1.5 %shard_map.69 = bf16[64,1024]{1,0:T(8,128)(2,1)} custom-call(bf16[64,32,128]{2,1,0:T(8,128)(2,1)S(1)} %all_to_all.23.state_ref, bf16[64,1024]{1,0:T(8,128)(2,1)S(1)} %bitcast.5, bf16[9,64,256]{2,1,0:T(8,128)(2,1)S(1)} %copy-done.1, f32[1,64]{1,0:T(1,128)S(1)} %bitcast.6), custom_call_target="tpu_custom_call" | custom-call | tf_op jit(solution)/shard_map/pallas_call | solution.py:54
  (1 shorter events, 0.0 us)
Async XLA Ops:
  0.0 0.7 %copy-start.4 = (f32[32]{0:T(128)S(1)}, f32[32]{0:T(128)}, u32[]{:S(2)}) copy-start(f32[32]{0:T(128)} %param.7) | copy-start | bytes 388
  0.0 0.9 %copy-start.2 = (bf16[1,64,1024]{2,1,0:T(8,128)(2,1)S(1)}, bf16[1,64,1024]{2,1,0:T(8,128)(2,1)}, u32[]{:S(2)}) copy-start(bf16[1,64,1024]{2,1,0:T(8,128)(2,1)} %param.6) | copy-start | bytes 393220
  0.7 19.9 %copy-start = (bf16[9,256,512]{2,1,0:T(8,128)(2,1)S(1)}, bf16[9,256,512]{2,1,0:T(8,128)(2,1)}, u32[]{:S(2)}) copy-start(bf16[9,256,512]{2,1,0:T(8,128)(2,1)} %weight_ref.2) | copy-start | bytes 7077892
  20.6 44.5 %copy-start.1 = (bf16[9,64,256]{2,1,0:T(8,128)(2,1)S(1)}, bf16[9,64,256]{2,1,0:T(8,128)(2,1)}, u32[]{:S(2)}) copy-start(bf16[9,64,256]{2,1,0:T(8,128)(2,1)} %weight_ref.3) | copy-start | bytes 884740
  20.6 44.5 %copy-start.3 = (f32[64]{0:T(128)S(1)}, f32[64]{0:T(128)}, u32[]{:S(2)}) copy-start(f32[64]{0:T(128)} %param.11) | copy-start | bytes 772

commit v9 on v8

--- a/solution.py
+++ b/solution.py
@@ -46,6 +46,25 @@
     lane = lanes_of(tile.shape)
     inside = (lane >= at) & (lane < at + 3)
     return jnp.sum(jnp.where(inside, tile.astype(F32), 0.0), axis=-1, keepdims=True)
+
+
+def diagonal(n):
+    return lax.broadcasted_iota(jnp.int32, (n, TILE), 0) == lanes_of((n, TILE))
+
+
+def lay_rows(column):
+    n = column.shape[0]
+    at = lax.broadcasted_iota(jnp.int32, (16, TILE), 0)
+    tile = jnp.zeros((16, TILE), F32)
+    for r, piece in enumerate(pieces(column)):
+        row = jnp.sum(jnp.where(diagonal(n), piece, 0.0), axis=0, keepdims=True)
+        tile = jnp.where(at == r, row, tile)
+    return tile.astype(BF)
+
+
+def read_rows(tile, n):
+    row = jnp.sum(tile.astype(F32), axis=0, keepdims=True)
+    return jnp.sum(jnp.where(diagonal(n), row, 0.0), axis=1, keepdims=True)
 
 
 def call(kernel, outs, *operands, places=None, scratch=(), vmem=32, cost=None):
@@ -128,45 +147,46 @@
     decay = jnp.exp(-jnp.concatenate(rates, axis=0) * step)
     inject = jnp.sqrt(1.0 - decay * decay)
     scaled = (inject * total).astype(BF)
-    meta = spread(decay, 0, (states, TILE)).astype(BF)
-    group, part, _ = out_ref.shape
+    part = states // len(part_order)
     for at, g in enumerate(part_order):
-        out_ref[at, :, :TILE] = scaled[g * part : (g + 1) * part]
-        out_ref[at, :, TILE:] = meta[g * part : (g + 1) * part]
+        out_ref[at, :part] = scaled[g * part : (g + 1) * part]
+        out_ref[at, part:] = lay_rows(decay[g * part : (g + 1) * part])
 
 
 def finish_group(order, driven_ref, out_ref):
-    frames, part, _ = driven_ref.shape
+    frames, height, _ = driven_ref.shape
+    part = height - 16
     state = None
     through = None
     for f in range(frames):
         at = order.index(f)
-        decay = collect(driven_ref[at, :, TILE:], 0)
-        value = driven_ref[at, :, :TILE].astype(F32)
+        decay = read_rows(driven_ref[at, part:], part)
+        value = driven_ref[at, :part].astype(F32)
         state = value if f == 0 else decay * state + value
         through = decay if f == 0 else decay * through
     final = state.astype(BF)
-    meta = spread(through, 0, (part, TILE)).astype(BF)
+    meta = lay_rows(through)
     for g in range(out_ref.shape[0]):
-        out_ref[g, :, :TILE] = final
-        out_ref[g, :, TILE:] = meta
+        out_ref[g, :part] = final
+        out_ref[g, part:] = meta
 
 
 def run_group(order, frame_order, spread_order, final_ref, driven_ref, out_ref):
     groups = final_ref.shape[0]
-    frames, part, _ = driven_ref.shape
+    frames, height, _ = driven_ref.shape
+    part = height - 16
     at = lax.axis_index("y")
     state = jnp.zeros((part, TILE), F32)
     for g in range(groups):
         source = order.index(g)
-        through = collect(final_ref[source, :, TILE:], 0)
-        moved = through * state + final_ref[source, :, :TILE].astype(F32)
+        through = read_rows(final_ref[source, part:], part)
+        moved = through * state + final_ref[source, :part].astype(F32)
         state = jnp.where(g < at, moved, state)
     copies = out_ref.shape[0] // frames
     for f in range(frames):
         source = frame_order.index(f)
-        decay = collect(driven_ref[source, :, TILE:], 0)
-        state = decay * state + driven_ref[source, :, :TILE].astype(F32)
+        decay = read_rows(driven_ref[source, part:], part)
+        state = decay * state + driven_ref[source, :part].astype(F32)
         rounded = state.astype(BF)
         for c in range(copies):
             out_ref[spread_order.index(f * copies + c)] = rounded
@@ -246,12 +266,12 @@
     rows = exchange(cut, "chan", Z_ORDER)
     driven = call(
         functools.partial(drive, Z_ORDER, X_ORDER),
-        shape((members, part, 2 * TILE), BF),
+        shape((members, part + 16, TILE), BF),
         rows,
         in_kernel,
     )
     driven = exchange(driven, "xc", X_ORDER)
-    final = call(functools.partial(finish_group, X_ORDER), shape((groups, part, 2 * TILE), BF), driven)
+    final = call(functools.partial(finish_group, X_ORDER), shape((groups, part + 16, TILE), BF), driven)
     final = exchange(final, "y", Y_ORDER)
     state = call(
         functools.partial(run_group, Y_ORDER, X_ORDER, S_ORDER),

time: 66.9 us -> 66 us (0.987)
  blocking collectives: 62.8 us -> 61.9 us
    all_to_all x4, blocking collectives: 62.8 us -> 61.9 us  [exchange(): return lax.all_to_all(x, axis, 0, 0, axis_index_groups=[order], tiled=True)]
where the time goes in v9:
time: 66 us; the launch traced here: 65.7 us
  blocking collectives  61.9 us (94%)
  Pallas kernels  2.9 us (4%)
  between operations  0.74 us (1%)
    all_to_all x4, blocking collectives, exchange(): return lax.all_to_all(x, axis, 0, 0, axis_index_groups=[order], tiled=True)  61.9 us
    pallas_call x6, Pallas kernels, call(): pl.pallas_call(kernel, out_shape=outs, in_specs=specs, out_specs=pl.Block...  2.9 us

profile of v9, /device:TPU:1, one launch (start us, length us, event | category | flops | bytes accessed | tf_op | source)
XLA Modules:
  0.0 65.7 jit_solution(2707849632452086979)
XLA Ops:
  0.0 0.0 copy-start.4
  0.0 0.0 copy-start.2
  0.7 0.0 copy-start
  0.7 0.0 copy-done.4
  0.7 0.2 copy-done.2
  0.9 0.1 shard_map.65
  1.1 19.6 %all_to_all.20.rows_ref = bf16[8,112,128]{2,1,0:T(8,128)(2,1)S(1)} all-to-all(bf16[8,112,128]{2,1,0:T(8,128)(2,1)S(1)} %shard_map.65), channel_id=1, replica_groups={{5,1,7,3,4,2,6,0},{13,9,15,11,12,10,14,8},{21,17,23,19,20,18,22,16},{29..., dimensions={0} | all-to-all | bytes 458752 | tf_op jit(solution)/shard_map/all_to_all | solution.py:239
  20.6 0.0 copy-done
  20.6 0.0 copy-start.1
  20.6 0.0 copy-start.3
  20.6 1.0 %shard_map.66 = bf16[8,48,128]{2,1,0:T(8,128)(2,1)S(1)} custom-call(bf16[8,112,128]{2,1,0:T(8,128)(2,1)S(1)} %all_to_all.20.rows_ref, bf16[9,256,512]{2,1,0:T(8,128)(2,1)S(1)} %copy-done), custom_call_target="tpu_custom_call" | custom-call | tf_op jit(solution)/shard_map/pallas_call | solution.py:73
  21.7 8.3 %all_to_all.21.driven_ref = bf16[8,48,128]{2,1,0:T(8,128)(2,1)S(1)} all-to-all(bf16[8,48,128]{2,1,0:T(8,128)(2,1)S(1)} %shard_map.66), channel_id=1, replica_groups={{40,56,8,24,32,48,0,16},{41,57,9,25,33,49,1,17},{42,58,10,26,34,50,2,18..., dimensions={0} | all-to-all | bytes 196608 | tf_op jit(solution)/shard_map/all_to_all | solution.py:239
  29.9 0.1 shard_map.67
  30.1 10.7 %all_to_all.22.final_ref = bf16[8,48,128]{2,1,0:T(8,128)(2,1)S(1)} all-to-all(bf16[8,48,128]{2,1,0:T(8,128)(2,1)S(1)} %shard_map.67), channel_id=1, replica_groups={{256,128,384,64,320,192,448,0},{257,129,385,65,321,193,449,1},{258,130,..., dimensions={0} | all-to-all | bytes 196608 | tf_op jit(solution)/shard_map/all_to_all | solution.py:239
  40.8 0.2 shard_map.68
  41.0 23.3 %all_to_all.23.state_ref = bf16[64,32,128]{2,1,0:T(8,128)(2,1)S(1)} all-to-all(bf16[64,32,128]{2,1,0:T(8,128)(2,1)S(1)} %shard_map.68), channel_id=1, replica_groups={{44,46,45,43,47,60,62,61,59,63,4,6,5,3,7,20,22,21,19,23,36,38,37,35,39,..., dimensions={0} | all-to-all | bytes 1048576 | tf_op jit(solution)/shard_map/all_to_all | solution.py:239
  64.2 0.0 copy-done.1
  64.2 0.0 copy-done.3
  64.2 1.5 %shard_map.69 = bf16[64,1024]{1,0:T(8,128)(2,1)} custom-call(bf16[64,32,128]{2,1,0:T(8,128)(2,1)S(1)} %all_to_all.23.state_ref, bf16[64,1024]{1,0:T(8,128)(2,1)S(1)} %bitcast.5, bf16[9,64,256]{2,1,0:T(8,128)(2,1)S(1)} %copy-done.1, f32[1,64]{1,0:T(1,128)S(1)} %bitcast.6), custom_call_target="tpu_custom_call" | custom-call | tf_op jit(solution)/shard_map/pallas_call | solution.py:73
  (1 shorter events, 0.0 us)
Async XLA Ops:
  0.0 0.7 %copy-start.4 = (f32[32]{0:T(128)S(1)}, f32[32]{0:T(128)}, u32[]{:S(2)}) copy-start(f32[32]{0:T(128)} %param.7) | copy-start | bytes 388
  0.0 0.9 %copy-start.2 = (bf16[1,64,1024]{2,1,0:T(8,128)(2,1)S(1)}, bf16[1,64,1024]{2,1,0:T(8,128)(2,1)}, u32[]{:S(2)}) copy-start(bf16[1,64,1024]{2,1,0:T(8,128)(2,1)} %param.6) | copy-start | bytes 393220
  0.7 19.9 %copy-start = (bf16[9,256,512]{2,1,0:T(8,128)(2,1)S(1)}, bf16[9,256,512]{2,1,0:T(8,128)(2,1)}, u32[]{:S(2)}) copy-start(bf16[9,256,512]{2,1,0:T(8,128)(2,1)} %weight_ref.2) | copy-start | bytes 7077892
  20.6 43.6 %copy-start.1 = (bf16[9,64,256]{2,1,0:T(8,128)(2,1)S(1)}, bf16[9,64,256]{2,1,0:T(8,128)(2,1)}, u32[]{:S(2)}) copy-start(bf16[9,64,256]{2,1,0:T(8,128)(2,1)} %weight_ref.3) | copy-start | bytes 884740
  20.6 43.6 %copy-start.3 = (f32[64]{0:T(128)S(1)}, f32[64]{0:T(128)}, u32[]{:S(2)}) copy-start(f32[64]{0:T(128)} %param.11) | copy-start | bytes 772

commit v10 on v9

--- a/solution.py
+++ b/solution.py
@@ -54,8 +54,8 @@
 
 def lay_rows(column):
     n = column.shape[0]
-    at = lax.broadcasted_iota(jnp.int32, (16, TILE), 0)
-    tile = jnp.zeros((16, TILE), F32)
+    at = lax.broadcasted_iota(jnp.int32, (8, TILE), 0)
+    tile = jnp.zeros((8, TILE), F32)
     for r, piece in enumerate(pieces(column)):
         row = jnp.sum(jnp.where(diagonal(n), piece, 0.0), axis=0, keepdims=True)
         tile = jnp.where(at == r, row, tile)
@@ -94,10 +94,11 @@
     near = lane[:half]
     outer = (near < ROW) | (near >= TILE - ROW)
     rate = to_column(rate_ref[...])
-    part = rate.shape[0] // 2
-    tile = (part, TILE)
-    meta = spread(rate[:part], 0, tile) + spread(rate[part:], 3, tile)
-    meta = (meta + spread(jnp.broadcast_to(step_ref[:1, :1], (part, 1)), 6, tile)).astype(BF)
+    at = lax.broadcasted_iota(jnp.int32, (8, TILE), 0)
+    meta = lay_rows(rate).astype(F32)
+    for r, piece in enumerate(pieces(step_ref[:1])):
+        meta = jnp.where(at == r + 3, piece, meta)
+    meta = meta.astype(BF)
     for at, b in enumerate(order):
         out_ref[at, :channels] = frame_ref[:, b * TILE : (b + 1) * TILE]
         side = jnp.zeros((channels, TILE), F32)
@@ -125,9 +126,9 @@
         packed = rows_ref[at, channels : channels + half]
         sides += [packed, roll_lanes(packed.astype(F32), TILE // 2).astype(BF)]
         meta = rows_ref[at, channels + half :]
-        rates += [collect(meta, 0), collect(meta, 3)]
+        rates.append(read_rows(meta[:3], states // blocks))
     side = jnp.concatenate(sides, axis=0)
-    step = collect(rows_ref[0, channels + half : channels + half + 8], 6)[:1]
+    step = jnp.sum(rows_ref[0, channels + half + 3 : channels + half + 6].astype(F32), axis=0, keepdims=True)[:, :1]
     lane = lanes_of(main.shape)
     column = lanes_of((states, TILE)) % ROW
     total = None
@@ -155,7 +156,7 @@
 
 def finish_group(order, driven_ref, out_ref):
     frames, height, _ = driven_ref.shape
-    part = height - 16
+    part = height - 8
     state = None
     through = None
     for f in range(frames):
@@ -174,7 +175,7 @@
 def run_group(order, frame_order, spread_order, final_ref, driven_ref, out_ref):
     groups = final_ref.shape[0]
     frames, height, _ = driven_ref.shape
-    part = height - 16
+    part = height - 8
     at = lax.axis_index("y")
     state = jnp.zeros((part, TILE), F32)
     for g in range(groups):
@@ -257,7 +258,7 @@
     )
     cut = call(
         functools.partial(cut_rows, Z_ORDER),
-        shape((blocks, channels + channels // 2 + rates // 2, TILE), BF),
+        shape((blocks, channels + channels // 2 + 8, TILE), BF),
         step,
         frame,
         decay_rate[None],
@@ -266,12 +267,12 @@
     rows = exchange(cut, "chan", Z_ORDER)
     driven = call(
         functools.partial(drive, Z_ORDER, X_ORDER),
-        shape((members, part + 16, TILE), BF),
+        shape((members, part + 8, TILE), BF),
         rows,
         in_kernel,
     )
     driven = exchange(driven, "xc", X_ORDER)
-    final = call(functools.partial(finish_group, X_ORDER), shape((groups, part + 16, TILE), BF), driven)
+    final = call(functools.partial(finish_group, X_ORDER), shape((groups, part + 8, TILE), BF), driven)
     final = exchange(final, "y", Y_ORDER)
     state = call(
         functools.partial(run_group, Y_ORDER, X_ORDER, S_ORDER),

time: 66 us -> 65.2 us (0.988)
  blocking collectives: 61.9 us -> 61.1 us
    all_to_all x4, blocking collectives: 61.9 us -> 61.1 us  [exchange(): return lax.all_to_all(x, axis, 0, 0, axis_index_groups=[order], tiled=True)]
where the time goes in v10:
time: 65.2 us; the launch traced here: 65 us
  blocking collectives  61.1 us (94%)
  Pallas kernels  2.88 us (4%)
  between operations  0.74 us (1%)
    all_to_all x4, blocking collectives, exchange(): return lax.all_to_all(x, axis, 0, 0, axis_index_groups=[order], tiled=True)  61.1 us
    pallas_call x6, Pallas kernels, call(): pl.pallas_call(kernel, out_shape=outs, in_specs=specs, out_specs=pl.Block...  2.88 us

profile of v10, /device:TPU:1, one launch (start us, length us, event | category | flops | bytes accessed | tf_op | source)
XLA Modules:
  0.0 65.0 jit_solution(4166357978654392128)
XLA Ops:
  0.0 0.0 copy-start.4
  0.0 0.0 copy-start.2
  0.7 0.0 copy-start
  0.7 0.0 copy-done.4
  0.7 0.2 copy-done.2
  0.9 0.1 shard_map.65
  1.0 19.2 %all_to_all.20.rows_ref = bf16[8,104,128]{2,1,0:T(8,128)(2,1)S(1)} all-to-all(bf16[8,104,128]{2,1,0:T(8,128)(2,1)S(1)} %shard_map.65), channel_id=1, replica_groups={{5,1,7,3,4,2,6,0},{13,9,15,11,12,10,14,8},{21,17,23,19,20,18,22,16},{29..., dimensions={0} | all-to-all | bytes 425984 | tf_op jit(solution)/shard_map/all_to_all | solution.py:240
  20.2 0.0 copy-done
  20.2 0.0 copy-start.1
  20.2 0.0 copy-start.3
  20.2 1.0 %shard_map.66 = bf16[8,40,128]{2,1,0:T(8,128)(2,1)S(1)} custom-call(bf16[8,104,128]{2,1,0:T(8,128)(2,1)S(1)} %all_to_all.20.rows_ref, bf16[9,256,512]{2,1,0:T(8,128)(2,1)S(1)} %copy-done), custom_call_target="tpu_custom_call" | custom-call | tf_op jit(solution)/shard_map/pallas_call | solution.py:73
  21.2 8.3 %all_to_all.21.driven_ref = bf16[8,40,128]{2,1,0:T(8,128)(2,1)S(1)} all-to-all(bf16[8,40,128]{2,1,0:T(8,128)(2,1)S(1)} %shard_map.66), channel_id=1, replica_groups={{40,56,8,24,32,48,0,16},{41,57,9,25,33,49,1,17},{42,58,10,26,34,50,2,18..., dimensions={0} | all-to-all | bytes 163840 | tf_op jit(solution)/shard_map/all_to_all | solution.py:240
  29.5 0.1 shard_map.67
  29.7 10.5 %all_to_all.22.final_ref = bf16[8,40,128]{2,1,0:T(8,128)(2,1)S(1)} all-to-all(bf16[8,40,128]{2,1,0:T(8,128)(2,1)S(1)} %shard_map.67), channel_id=1, replica_groups={{256,128,384,64,320,192,448,0},{257,129,385,65,321,193,449,1},{258,130,..., dimensions={0} | all-to-all | bytes 163840 | tf_op jit(solution)/shard_map/all_to_all | solution.py:240
  40.2 0.2 shard_map.68
  40.3 23.2 %all_to_all.23.state_ref = bf16[64,32,128]{2,1,0:T(8,128)(2,1)S(1)} all-to-all(bf16[64,32,128]{2,1,0:T(8,128)(2,1)S(1)} %shard_map.68), channel_id=1, replica_groups={{44,46,45,43,47,60,62,61,59,63,4,6,5,3,7,20,22,21,19,23,36,38,37,35,39,..., dimensions={0} | all-to-all | bytes 1048576 | tf_op jit(solution)/shard_map/all_to_all | solution.py:240
  63.5 0.0 copy-done.1
  63.5 0.0 copy-done.3
  63.5 1.5 %shard_map.69 = bf16[64,1024]{1,0:T(8,128)(2,1)} custom-call(bf16[64,32,128]{2,1,0:T(8,128)(2,1)S(1)} %all_to_all.23.state_ref, bf16[64,1024]{1,0:T(8,128)(2,1)S(1)} %bitcast.5, bf16[9,64,256]{2,1,0:T(8,128)(2,1)S(1)} %copy-done.1, f32[1,64]{1,0:T(1,128)S(1)} %bitcast.6), custom_call_target="tpu_custom_call" | custom-call | tf_op jit(solution)/shard_map/pallas_call | solution.py:73
  (1 shorter events, 0.0 us)
Async XLA Ops:
  0.0 0.7 %copy-start.4 = (f32[32]{0:T(128)S(1)}, f32[32]{0:T(128)}, u32[]{:S(2)}) copy-start(f32[32]{0:T(128)} %param.7) | copy-start | bytes 388
  0.0 0.9 %copy-start.2 = (bf16[1,64,1024]{2,1,0:T(8,128)(2,1)S(1)}, bf16[1,64,1024]{2,1,0:T(8,128)(2,1)}, u32[]{:S(2)}) copy-start(bf16[1,64,1024]{2,1,0:T(8,128)(2,1)} %param.6) | copy-start | bytes 393220
  0.7 19.5 %copy-start = (bf16[9,256,512]{2,1,0:T(8,128)(2,1)S(1)}, bf16[9,256,512]{2,1,0:T(8,128)(2,1)}, u32[]{:S(2)}) copy-start(bf16[9,256,512]{2,1,0:T(8,128)(2,1)} %weight_ref.2) | copy-start | bytes 7077892
  20.2 43.3 %copy-start.1 = (bf16[9,64,256]{2,1,0:T(8,128)(2,1)S(1)}, bf16[9,64,256]{2,1,0:T(8,128)(2,1)}, u32[]{:S(2)}) copy-start(bf16[9,64,256]{2,1,0:T(8,128)(2,1)} %weight_ref.3) | copy-start | bytes 884740
  20.2 43.3 %copy-start.3 = (f32[64]{0:T(128)S(1)}, f32[64]{0:T(128)}, u32[]{:S(2)}) copy-start(f32[64]{0:T(128)} %param.11) | copy-start | bytes 772

commit v11 on v10

--- a/solution.py
+++ b/solution.py
@@ -67,14 +67,14 @@
     return jnp.sum(jnp.where(diagonal(n), row, 0.0), axis=1, keepdims=True)
 
 
-def call(kernel, outs, *operands, places=None, scratch=(), vmem=32, cost=None):
+def call(kernel, outs, *operands, places=None, out_place=pltpu.VMEM, scratch=(), vmem=32, cost=None):
     places = places or (pltpu.VMEM,) * len(operands)
     specs = [pl.BlockSpec(memory_space=place) for place in places]
     return pl.pallas_call(
         kernel,
         out_shape=outs,
         in_specs=specs,
-        out_specs=pl.BlockSpec(memory_space=pltpu.VMEM),
+        out_specs=pl.BlockSpec(memory_space=out_place),
         scratch_shapes=scratch,
         cost_estimate=cost,
         compiler_params=pltpu.CompilerParams(vmem_limit_bytes=vmem << 20),
@@ -193,7 +193,7 @@
             out_ref[spread_order.index(f * copies + c)] = rounded
 
 
-def finish(order, state_ref, frame_ref, weight_ref, gain_ref, out_ref):
+def finish(order, state_ref, frame_ref, weight_ref, gain_ref, out_ref, done_ref, sems):
     channels, cells = frame_ref.shape
     blocks = cells // TILE
     states = weight_ref.shape[2]
@@ -203,31 +203,42 @@
         return jnp.concatenate([state_ref[order.index(p * blocks + b)] for p in range(parts)], axis=0)
 
     source = jnp.concatenate([rows(b) for b in range(blocks)], axis=1)
-    weight = weight_ref[...].reshape(9 * channels, states)
-    taps = jnp.dot(weight, source, preferred_element_type=F32)
-    lane = lanes_of((channels, TILE))
-    column = lane % ROW
-    gain = to_column(gain_ref[...])
-
-    def row(i, b):
-        def tap(j):
-            at = (3 * i + j) * channels
-            return taps[at : at + channels, b * TILE : (b + 1) * TILE]
-
-        left = jnp.where(column > 0, roll_lanes(tap(0), 1), 0.0)
-        right = jnp.where(column < ROW - 1, roll_lanes(tap(2), -1), 0.0)
-        return tap(1) + left + right
-
-    down = [roll_lanes(row(0, b), ROW) for b in range(blocks)]
-    up = [roll_lanes(row(2, b), -ROW) for b in range(blocks)]
-    for b in range(blocks):
-        at = slice(b * TILE, (b + 1) * TILE)
-        before = down[b - 1] if b > 0 else 0.0
-        after = up[b + 1] if b + 1 < blocks else 0.0
-        total = row(1, b) + gain * frame_ref[:, at].astype(F32)
-        total = total + jnp.where(lane < ROW, before, down[b])
-        total = total + jnp.where(lane >= TILE - ROW, after, up[b])
-        out_ref[:, at] = jax.nn.gelu(total).astype(BF)
+    gains = to_column(gain_ref[...])
+    halves = 2
+    channels //= halves
+    copies = []
+    for half in range(halves):
+        top = half * channels
+        weight = weight_ref[:, top : top + channels].reshape(9 * channels, states)
+        taps = jnp.dot(weight, source, preferred_element_type=F32)
+        lane = lanes_of((channels, TILE))
+        column = lane % ROW
+        gain = gains[top : top + channels]
+
+        def row(i, b):
+            def tap(j):
+                at = (3 * i + j) * channels
+                return taps[at : at + channels, b * TILE : (b + 1) * TILE]
+
+            left = jnp.where(column > 0, roll_lanes(tap(0), 1), 0.0)
+            right = jnp.where(column < ROW - 1, roll_lanes(tap(2), -1), 0.0)
+            return tap(1) + left + right
+
+        down = [roll_lanes(row(0, b), ROW) for b in range(blocks)]
+        up = [roll_lanes(row(2, b), -ROW) for b in range(blocks)]
+        for b in range(blocks):
+            at = slice(b * TILE, (b + 1) * TILE)
+            before = down[b - 1] if b > 0 else 0.0
+            after = up[b + 1] if b + 1 < blocks else 0.0
+            total = row(1, b) + gain * frame_ref[top : top + channels, at].astype(F32)
+            total = total + jnp.where(lane < ROW, before, down[b])
+            total = total + jnp.where(lane >= TILE - ROW, after, up[b])
+            done_ref[top : top + channels, at] = jax.nn.gelu(total).astype(BF)
+        rows_at = pl.ds(top, channels)
+        copies.append(pltpu.make_async_copy(done_ref.at[rows_at], out_ref.at[rows_at], sems.at[half]))
+        copies[-1].start()
+    for copy in copies:
+        copy.wait()
 
 
 Z_ORDER = [5, 1, 7, 3, 4, 2, 6, 0]
@@ -288,6 +299,8 @@
         frame,
         out_kernel,
         skip_gain[None],
+        out_place=pltpu.HBM,
+        scratch=(pltpu.VMEM((channels, cells), BF), pltpu.SemaphoreType.DMA((2,))),
     )
     return out[None]
 

time: 65.2 us -> 65.3 us (level)
  no operation moved by 1% of the time
where the time goes in v11:
time: 65.3 us; the launch traced here: 65.1 us
  blocking collectives  61.1 us (94%)
  Pallas kernels  2.97 us (5%)
  between operations  0.74 us (1%)
    all_to_all x4, blocking collectives, exchange(): return lax.all_to_all(x, axis, 0, 0, axis_index_groups=[order], tiled=True)  61.1 us
    pallas_call x6, Pallas kernels, call(): pl.pallas_call(kernel, out_shape=outs, in_specs=specs, out_specs=pl.Block...  2.97 us

profile of v11, /device:TPU:1, one launch (start us, length us, event | category | flops | bytes accessed | tf_op | source)
XLA Modules:
  0.0 65.1 jit_solution(18298395571766799595)
XLA Ops:
  0.0 0.0 copy-start.4
  0.0 0.0 copy-start.2
  0.7 0.0 copy-start
  0.7 0.0 copy-done.4
  0.7 0.2 copy-done.2
  0.9 0.1 shard_map.65
  1.0 19.2 %all_to_all.20.rows_ref = bf16[8,104,128]{2,1,0:T(8,128)(2,1)S(1)} all-to-all(bf16[8,104,128]{2,1,0:T(8,128)(2,1)S(1)} %shard_map.65), channel_id=1, replica_groups={{5,1,7,3,4,2,6,0},{13,9,15,11,12,10,14,8},{21,17,23,19,20,18,22,16},{29..., dimensions={0} | all-to-all | bytes 425984 | tf_op jit(solution)/shard_map/all_to_all | solution.py:251
  20.2 0.0 copy-done
  20.2 0.0 copy-start.1
  20.2 0.0 copy-start.3
  20.2 1.0 %shard_map.66 = bf16[8,40,128]{2,1,0:T(8,128)(2,1)S(1)} custom-call(bf16[8,104,128]{2,1,0:T(8,128)(2,1)S(1)} %all_to_all.20.rows_ref, bf16[9,256,512]{2,1,0:T(8,128)(2,1)S(1)} %copy-done), custom_call_target="tpu_custom_call" | custom-call | tf_op jit(solution)/shard_map/pallas_call | solution.py:73
  21.2 8.3 %all_to_all.21.driven_ref = bf16[8,40,128]{2,1,0:T(8,128)(2,1)S(1)} all-to-all(bf16[8,40,128]{2,1,0:T(8,128)(2,1)S(1)} %shard_map.66), channel_id=1, replica_groups={{40,56,8,24,32,48,0,16},{41,57,9,25,33,49,1,17},{42,58,10,26,34,50,2,18..., dimensions={0} | all-to-all | bytes 163840 | tf_op jit(solution)/shard_map/all_to_all | solution.py:251
  29.5 0.1 shard_map.67
  29.7 10.5 %all_to_all.22.final_ref = bf16[8,40,128]{2,1,0:T(8,128)(2,1)S(1)} all-to-all(bf16[8,40,128]{2,1,0:T(8,128)(2,1)S(1)} %shard_map.67), channel_id=1, replica_groups={{256,128,384,64,320,192,448,0},{257,129,385,65,321,193,449,1},{258,130,..., dimensions={0} | all-to-all | bytes 163840 | tf_op jit(solution)/shard_map/all_to_all | solution.py:251
  40.2 0.2 shard_map.68
  40.3 23.2 %all_to_all.23.state_ref = bf16[64,32,128]{2,1,0:T(8,128)(2,1)S(1)} all-to-all(bf16[64,32,128]{2,1,0:T(8,128)(2,1)S(1)} %shard_map.68), channel_id=1, replica_groups={{44,46,45,43,47,60,62,61,59,63,4,6,5,3,7,20,22,21,19,23,36,38,37,35,39,..., dimensions={0} | all-to-all | bytes 1048576 | tf_op jit(solution)/shard_map/all_to_all | solution.py:251
  63.5 0.0 copy-done.1
  63.5 0.0 copy-done.3
  63.5 1.6 %shard_map.69 = bf16[64,1024]{1,0:T(8,128)(2,1)} custom-call(bf16[64,32,128]{2,1,0:T(8,128)(2,1)S(1)} %all_to_all.23.state_ref, bf16[64,1024]{1,0:T(8,128)(2,1)S(1)} %bitcast.5, bf16[9,64,256]{2,1,0:T(8,128)(2,1)S(1)} %copy-done.1, f32[1,64]{1,0:T(1,128)S(1)} %bitcast.6), custom_call_target="tpu_custom_call" | custom-call | tf_op jit(solution)/shard_map/pallas_call | solution.py:73
  (1 shorter events, 0.0 us)
Async XLA Ops:
  0.0 0.7 %copy-start.4 = (f32[32]{0:T(128)S(1)}, f32[32]{0:T(128)}, u32[]{:S(2)}) copy-start(f32[32]{0:T(128)} %param.7) | copy-start | bytes 388
  0.0 0.9 %copy-start.2 = (bf16[1,64,1024]{2,1,0:T(8,128)(2,1)S(1)}, bf16[1,64,1024]{2,1,0:T(8,128)(2,1)}, u32[]{:S(2)}) copy-start(bf16[1,64,1024]{2,1,0:T(8,128)(2,1)} %param.6) | copy-start | bytes 393220
  0.7 19.5 %copy-start = (bf16[9,256,512]{2,1,0:T(8,128)(2,1)S(1)}, bf16[9,256,512]{2,1,0:T(8,128)(2,1)}, u32[]{:S(2)}) copy-start(bf16[9,256,512]{2,1,0:T(8,128)(2,1)} %weight_ref.2) | copy-start | bytes 7077892
  20.2 43.3 %copy-start.1 = (bf16[9,64,256]{2,1,0:T(8,128)(2,1)S(1)}, bf16[9,64,256]{2,1,0:T(8,128)(2,1)}, u32[]{:S(2)}) copy-start(bf16[9,64,256]{2,1,0:T(8,128)(2,1)} %weight_ref.3) | copy-start | bytes 884740
  20.2 43.3 %copy-start.3 = (f32[64]{0:T(128)S(1)}, f32[64]{0:T(128)}, u32[]{:S(2)}) copy-start(f32[64]{0:T(128)} %param.11) | copy-start | bytes 772
